TPU v7x, 256 devices: a whole 4x4x8 slice. The times are simulated.
256 devices in a mesh: nodes: 16 (over z, core), feat: 16 (over y, x).
Axes of the slice: x: 4, y: 4, z: 8, core: 2. Of those that a mesh axis runs over, the one named last changes fastest.
Arguments:
- features: bfloat16 [262144, 1024], P('nodes', 'feat'), may hold values from -6 to 6
- tile_vals: bfloat16 [16, 16, 12, 128, 128], P('nodes'), may hold values from -0.375 to 0.375
- src_tile: int32 [16, 16, 12], P('nodes'), may hold values from 0 to 127
- dst_tile: int32 [16, 16, 12], P('nodes'), may hold values from 0 to 127
- counts: int32 [16, 16], P('nodes'), may hold values from 1 to 12, as said below
- weight: bfloat16 [2, 1024, 1024], replicated, may hold values from -0.125 to 0.125
Outputs:
- embedded: bfloat16 [262144, 1024], P('nodes', 'feat')
Inputs may be any that keep to these rules, and one draw needn't show every extreme that they name: `counts`: in every draw one destination block receives 12 used slots from every source block.
All inputs are finite; a program needn't handle non-finite values.
Results may differ from a plain program's by a relative error of at most 0.0085.
Values may be sent and summed in bfloat16 or wider, within the bound.
A program may use at most 192 MiB of HBM per device.

v0:
```python
import jax
import jax.numpy as jnp
from jax import lax
from jax.sharding import PartitionSpec as P


def on_device(features, tile_vals, src_tile, dst_tile, counts, weight):
    row_count, col_count = features.shape
    tile_size = tile_vals.shape[-1]
    owners = tile_vals.shape[1]
    slot_count = tile_vals.shape[2]
    model_width = weight.shape[1]
    blocks = row_count // tile_size
    panels = features.reshape(blocks, tile_size, col_count)
    picked = panels[src_tile[0]]
    partial_value = jnp.einsum(
        "ncij,ncjd->ncid", tile_vals[0], picked, preferred_element_type=jnp.float32
    )
    usable = lax.broadcasted_iota(jnp.int32, (owners, slot_count), 1) < counts[0][:, None]
    partial_value = jnp.where(usable[:, :, None, None], partial_value, 0.0).astype(jnp.bfloat16)
    arrived, targets = (
        lax.all_to_all(partial_value, "nodes", split_axis=0, concat_axis=0, tiled=True),
        lax.all_to_all(dst_tile[0], "nodes", split_axis=0, concat_axis=0, tiled=True),
    )
    onehot = (targets.reshape(1, -1) == lax.broadcasted_iota(jnp.int32, (blocks, 1), 0)).astype(
        jnp.bfloat16
    )
    aggregate = jnp.dot(
        onehot,
        arrived.reshape(owners * slot_count, tile_size * col_count),
        preferred_element_type=jnp.float32,
    )
    aggregate = aggregate.reshape(row_count, col_count).astype(jnp.bfloat16)
    wide_agg, wide_self = (
        lax.all_to_all(aggregate, "feat", split_axis=0, concat_axis=1, tiled=True),
        lax.all_to_all(features, "feat", split_axis=0, concat_axis=1, tiled=True),
    )
    hidden = jnp.dot(wide_agg, weight[0], preferred_element_type=jnp.float32)
    hidden = hidden + jnp.dot(wide_self, weight[1], preferred_element_type=jnp.float32)
    active = jnp.maximum(hidden, 0.0)
    row_total = jnp.sum(active * active, axis=1, keepdims=True)
    row_result = (active * lax.rsqrt(row_total / model_width + 1e-06)).astype(jnp.bfloat16)
    return lax.all_to_all(row_result, "feat", split_axis=1, concat_axis=0, tiled=True)


def solution(mesh):
    return jax.shard_map(
        on_device,
        mesh=mesh,
        in_specs=(
            P("nodes", "feat"),
            P("nodes", None, None, None, None),
            P("nodes", None, None),
            P("nodes", None, None),
            P("nodes", None),
            P(),
        ),
        out_specs=P("nodes", "feat"),
        check_vma=False,
    )
```

profile of v0, /device:TPU:1, one launch (start us, length us, event | category | flops | bytes accessed | tf_op | source)
XLA Modules:
  0.0 215.0 jit_solution(2699982227981059055)
XLA Ops:
  0.0 0.0 copy-start
  0.0 1.4 copy.35
  1.4 10.0 %all-to-all-start = ((s32[16,1,12]{2,1,0:T(1,128)}), s32[16,1,12]{2,1,0:T(1,128)S(1)}, u32[]{:S(2)}, u32[]{:S(2)}) async-start(s32[16,1,12]{2,1,0:T(1,128)} %copy.35), calls=%async_computation | async-start | bytes 16384 | tf_op jit(solution)/shard_map/all_to_all | solution.py:23
  11.4 2.2 %copy_bitcast_fusion.1 = bf16[128,128,64]{1,2,0:T(8,128)(2,1)S(1)} fusion(bf16[16384,64]{0,1:T(8,128)(2,1)} %param.6), kind=kLoop, calls=%fused_computation.10 | loop fusion | bytes 4194304 | tf_op jit(solution)/shard_map/reshape | solution.py:14
  13.6 0.0 copy-done
  13.6 0.1 copy.36
  13.7 0.1 reshape.86
  13.8 0.0 copy-done.1
  13.8 0.1 iota_compare_fusion.2
  13.9 2.7 %gather_fusion = bf16[192,128,64]{1,2,0:T(8,128)(2,1)} fusion(bf16[128,128,64]{1,2,0:T(8,128)(2,1)S(1)} %copy_bitcast_fusion.1, s32[1024]{0:T(1024)S(1)} %pad_clamp_fusion), kind=kCustom, calls=%fused_computation | custom fusion | bytes 6292224 | tf_op jit(solution)/shard_map/gather | solution.py:15
  16.6 9.8 %fusion.2 = bf16[16,12,128,64]{2,3,1,0:T(8,128)(2,1)} fusion(pred[16,12]{1,0:T(8,128)(4,1)S(1)} %iota_compare_fusion.2, bf16[16,12,128,64]{2,3,1,0:T(8,128)(2,1)} %bitcast.49, bf16[1,16,12,128,128]{4,3,2,1,0:T(8,128)(2,1)} %param.7), kind=kOutput, calls=%fused_computation.8 | convolution fusion | flops 405798912 | bytes 12583104 | tf_op jit(solution)/shard_map/ncij,ncjd->ncid/dot_general | solution.py:16
  26.4 0.0 all-to-all-done
  26.4 7.2 %all-to-all-start.1 = ((bf16[16,12,128,64]{2,3,1,0:T(8,128)(2,1)}), bf16[16,12,128,64]{2,3,1,0:T(8,128)(2,1)S(1)}, u32[]{:S(2)}, u32[]{:S(2)}) async-start(bf16[16,12,128,64]{2,3,1,0:T(8,128)(2,1)} %fusion.2), calls=%async_computation.1 | async-start | bytes 6291456 | tf_op jit(solution)/shard_map/all_to_all | solution.py:22
  33.6 3.1 %copy.47 = bf16[8,16,8,1024]{3,2,0,1:T(8,128)(2,1)} copy(bf16[8,16,8,1024]{3,2,1,0:T(8,128)(2,1)} %bitcast.50) | data formatting | bytes 4194304 | tf_op jit(solution)/shard_map/all_to_all | solution.py:36
  36.8 67.8 %all-to-all-done.1 = bf16[16,12,128,64]{2,3,1,0:T(8,128)(2,1)S(1)} async-done(((bf16[16,12,128,64]{2,3,1,0:T(8,128)(2,1)}), bf16[16,12,128,64]{2,3,1,0:T(8,128)(2,1)S(1)}, u32[]{:S(2)}, u32[]{:S(2)}) %all-to-all-start.1) | async-done | bytes 3145760 | tf_op jit(solution)/shard_map/all_to_all | solution.py:22
  104.6 6.8 %all-to-all-start.3 = ((bf16[16,1024,64]{1,2,0:T(8,128)(2,1)}), bf16[16,1024,64]{1,2,0:T(8,128)(2,1)}, u32[]{:S(2)}, u32[]{:S(2)}) async-start(bf16[16,1024,64]{1,2,0:T(8,128)(2,1)} %bitcast.51), calls=%async_computation.3 | async-start | bytes 4194304 | tf_op jit(solution)/shard_map/all_to_all | solution.py:36
  111.4 0.5 broadcast.46
  111.9 0.6 reduce.3
  112.5 0.1 eq.15
  112.6 4.5 %copy.38 = bf16[16,12,128,64]{3,2,1,0:T(8,128)(2,1)} copy(bf16[16,12,128,64]{2,3,1,0:T(8,128)(2,1)S(1)} %all-to-all-done.1) | data formatting | bytes 6291456 | tf_op jit(solution)/shard_map/all_to_all | solution.py:22
  117.1 7.9 %reshape.83 = bf16[192,8192]{1,0:T(8,128)(2,1)S(1)} reshape(bf16[16,12,128,64]{3,2,1,0:T(8,128)(2,1)} %copy.38) | data formatting | bytes 6291456 | tf_op jit(solution)/shard_map/reshape | solution.py:30
  125.0 2.0 convolution_convert_fusion
  127.1 6.9 %convert_element_type.20 = bf16[16,1024,64]{2,1,0:T(8,128)(2,1)} reshape(bf16[128,8192]{1,0:T(8,128)(2,1)} %convolution_convert_fusion) | data formatting | bytes 4194304 | tf_op jit(solution)/shard_map/convert_element_type | solution.py:33
  133.9 4.8 %copy.39 = bf16[16,1024,64]{1,2,0:T(8,128)(2,1)} copy(bf16[16,1024,64]{2,1,0:T(8,128)(2,1)} %convert_element_type.20) | data formatting | bytes 4194304 | tf_op jit(solution)/shard_map/convert_element_type | solution.py:33
  138.7 2.7 %all-to-all-done.3 = bf16[16,1024,64]{1,2,0:T(8,128)(2,1)} async-done(((bf16[16,1024,64]{1,2,0:T(8,128)(2,1)}), bf16[16,1024,64]{1,2,0:T(8,128)(2,1)}, u32[]{:S(2)}, u32[]{:S(2)}) %all-to-all-start.3) | async-done | bytes 2097184 | tf_op jit(solution)/shard_map/all_to_all | solution.py:36
  141.4 4.5 %all-to-all-start.2 = ((bf16[16,1024,64]{1,2,0:T(8,128)(2,1)}), bf16[16,1024,64]{1,2,0:T(8,128)(2,1)S(1)}, u32[]{:S(2)}, u32[]{:S(2)}) async-start(bf16[16,1024,64]{1,2,0:T(8,128)(2,1)} %copy.39), calls=%async_computation.2 | async-start | bytes 4194304 | tf_op jit(solution)/shard_map/all_to_all | solution.py:35
  146.0 6.5 %fusion.5 = f32[1024,1024]{0,1:T(8,128)} fusion(bf16[1024,1024]{0,1:T(8,128)(2,1)} %bitcast.10, bf16[2,1024,1024]{2,1,0:T(8,128)(2,1)} %param.11), kind=kOutput, calls=%fused_computation.11 | convolution fusion | flops 2147483648 | bytes 8388608 | tf_op jit(solution)/shard_map/dot_general | solution.py:39
  152.5 22.4 %all-to-all-done.2 = bf16[16,1024,64]{1,2,0:T(8,128)(2,1)S(1)} async-done(((bf16[16,1024,64]{1,2,0:T(8,128)(2,1)}), bf16[16,1024,64]{1,2,0:T(8,128)(2,1)S(1)}, u32[]{:S(2)}, u32[]{:S(2)}) %all-to-all-start.2) | async-done | bytes 2097184 | tf_op jit(solution)/shard_map/all_to_all | solution.py:35
  174.9 5.5 %multiply_reduce_fusion = (f32[1024]{0:T(1024)S(1)}, f32[1024,1024]{0,1:T(8,128)S(1)}) fusion(f32[1024,1024]{0,1:T(8,128)} %fusion.5, bf16[1024,1024]{0,1:T(8,128)(2,1)S(1)} %bitcast.54, bf16[2,1024,1024]{2,1,0:T(8,128)(2,1)} %param.11), kind=kOutput, calls=%fused_computation.6 | convolution fusion | flops 2151676928 | bytes 12587008 | tf_op jit(solution)/shard_map/dot_general | solution.py:38
  180.4 0.6 multiply_convert_fusion
  181.0 32.5 %all_to_all.68 = bf16[1024,16,64]{0,2,1:T(8,128)(2,1)S(1)} all-to-all(bf16[1024,16,64]{0,2,1:T(8,128)(2,1)S(1)} %bitcast.53), channel_id=1, replica_groups=mesh['nodes'=16,'feat'=16] {'feat'}, dimensions={1} | all-to-all | bytes 4194304 | tf_op jit(solution)/shard_map/all_to_all | solution.py:43
  213.5 1.5 copy.44
  (4 shorter events, 0.0 us)
Async XLA Ops:
  0.0 13.6 %copy-start = (s32[1,16,12]{1,0,2:T(1,128)S(1)}, s32[1,16,12]{1,0,2:T(1,128)}, u32[]{:S(2)}) copy-start(s32[1,16,12]{1,0,2:T(1,128)} %param.8) | copy-start | bytes 2308
  0.0 13.8 %copy-start.1 = (s32[1,16]{1,0:T(1,128)S(1)}, s32[1,16]{1,0:T(1,128)}, u32[]{:S(2)}) copy-start(s32[1,16]{1,0:T(1,128)} %param.10) | copy-start | bytes 196
  1.4 25.0 %all-to-all-start = ((s32[16,1,12]{2,1,0:T(1,128)}), s32[16,1,12]{2,1,0:T(1,128)S(1)}, u32[]{:S(2)}, u32[]{:S(2)}) async-start(s32[16,1,12]{2,1,0:T(1,128)} %copy.35), calls=%async_computation | async-start | bytes 16384 | tf_op jit(solution)/shard_map/all_to_all | solution.py:23
  26.4 78.2 %all-to-all-start.1 = ((bf16[16,12,128,64]{2,3,1,0:T(8,128)(2,1)}), bf16[16,12,128,64]{2,3,1,0:T(8,128)(2,1)S(1)}, u32[]{:S(2)}, u32[]{:S(2)}) async-start(bf16[16,12,128,64]{2,3,1,0:T(8,128)(2,1)} %fusion.2), calls=%async_computation.1 | async-start | bytes 6291456 | tf_op jit(solution)/shard_map/all_to_all | solution.py:22
  104.6 36.8 %all-to-all-start.3 = ((bf16[16,1024,64]{1,2,0:T(8,128)(2,1)}), bf16[16,1024,64]{1,2,0:T(8,128)(2,1)}, u32[]{:S(2)}, u32[]{:S(2)}) async-start(bf16[16,1024,64]{1,2,0:T(8,128)(2,1)} %bitcast.51), calls=%async_computation.3 | async-start | bytes 4194304 | tf_op jit(solution)/shard_map/all_to_all | solution.py:36
  141.4 33.5 %all-to-all-start.2 = ((bf16[16,1024,64]{1,2,0:T(8,128)(2,1)}), bf16[16,1024,64]{1,2,0:T(8,128)(2,1)S(1)}, u32[]{:S(2)}, u32[]{:S(2)}) async-start(bf16[16,1024,64]{1,2,0:T(8,128)(2,1)} %copy.39), calls=%async_computation.2 | async-start | bytes 4194304 | tf_op jit(solution)/shard_map/all_to_all | solution.py:35
where the time goes:
time: 217 us; the launch traced here: 215 us
  waiting for transfers between devices  93 us (43%)
  local copies, waits for them, and re-layouts  35.7 us (16%)
  blocking collectives  32.5 us (15%)
  starting transfers between devices  28.6 us (13%)
  matrix products  23.8 us (11%)
    all_to_all x1, waiting for transfers between devices, on_device(): lax.all_to_all(partial_value, 'nodes', split_axis=0, concat_axis=0, tiled...  67.8 us
    all_to_all x1, blocking collectives, on_device(): lax.all_to_all(row_result, 'feat', split_axis=1, concat_axis=0, tiled=True)  32.5 us
    all_to_all x1, waiting for transfers between devices, on_device(): lax.all_to_all(aggregate, 'feat', split_axis=0, concat_axis=1, tiled=True)  22.4 us
    convert_element_type x2, local copies, waits for them, and re-layouts, on_device(): aggregate = aggregate.reshape(row_count, col_count).astype(jnp.bfloat16)  11.6 us
    all_to_all x1, starting transfers between devices, on_device(): lax.all_to_all(dst_tile[0], 'nodes', split_axis=0, concat_axis=0, tiled=T...  9.98 us
    dot_general x1, matrix products, on_device(): jnp.einsum('ncij,ncjd->ncid', tile_vals[0], picked, preferred_element_typ...  9.83 us
    reshape x1, local copies, waits for them, and re-layouts, on_device(): arrived.reshape(owners * slot_count, tile_size * col_count)  7.92 us
    all_to_all x1, starting transfers between devices, on_device(): lax.all_to_all(partial_value, 'nodes', split_axis=0, concat_axis=0, tiled...  7.23 us
  transfers between devices with their start and end apart: 4, of which 3 were waited for; matrix products, arithmetic and copies ran while one was open for 24% of the time, Pallas kernels for 0%

commit v1 on v0

v1 whole, which is shorter than its diff:
```python
import jax
import jax.numpy as jnp
from jax import lax
from jax.experimental import pallas as pl
from jax.experimental.pallas import tpu as pltpu
from jax.sharding import PartitionSpec as P

MESH = pl.DeviceIdType.MESH
BF16, F32 = jnp.bfloat16, jnp.float32
N = 16
F = 16
CAP = 12
T = 128
TILES = 128
C = 64
D = 1024
K = 4
SHARE = 1024

NT = (((1,), (1,)), ((), ()))


def order(me, step):
    return lax.rem(me + step, 16)


def back_order(me, step):
    return lax.rem(me + 16 - step, 16)


def spread(into_chunks):
    a = lax.broadcasted_iota(jnp.int32, (512, 512), 0)
    b = lax.broadcasted_iota(jnp.int32, (512, 512), 1)
    nat, chunk = (a, b) if into_chunks else (b, a)
    tl, h, k, r = nat // 128, (nat // 64) % 2, (nat // 16) % 4, nat % 16
    return (chunk == k * 128 + h * 64 + tl * 16 + r).astype(F32).astype(BF16)


def kernel(
    src_ref,
    dmsg_ref,
    xt_ref,
    a_ref,
    w_ref,
    out_ref,
    xbuf,
    xtile,
    abuf,
    wbuf,
    wt0,
    wt1,
    zsend,
    zrecv,
    dtgt,
    r32,
    g32,
    asend,
    arecv,
    srecv,
    selfp,
    hs,
    lhs,
    act,
    bsend,
    brecv,
    perm,
    onehot,
    xsem,
    asem,
    wsem,
    own_sem,
    d_ss,
    d_rs,
    s_ss,
    s_rs,
    z_ss,
    z_rs,
    g_ss,
    g_rs,
    b_ss,
    b_rs,
):
    n, f = lax.axis_index("nodes"), lax.axis_index("feat")

    def node(i):
        return (i, f)

    def col(i):
        return (n, i)

    x_copy = pltpu.make_async_copy(xt_ref, xbuf, xsem)
    x_copy.start()

    def a_copy(step):
        d = order(n, step)
        return pltpu.make_async_copy(a_ref.at[d], abuf.at[d], asem.at[d])

    @pl.loop(0, 16)
    def _(step):
        a_copy(lax.rem(step + 1, 16)).start()

    w_copy = pltpu.make_async_copy(w_ref, wbuf, wsem)
    w_copy.start()

    barrier = pltpu.get_barrier_semaphore()

    @pl.loop(1, 16)
    def _(step):
        pl.semaphore_signal(barrier, inc=1, device_id=node(order(n, step)), device_id_type=MESH)
        pl.semaphore_signal(barrier, inc=1, device_id=col(order(f, step)), device_id_type=MESH)

    pl.semaphore_wait(barrier, 30)

    def d_send(to):
        return pltpu.make_async_remote_copy(
            dmsg_ref.at[to], dtgt.at[n], d_ss.at[to], d_rs.at[n], device_id=node(to), device_id_type=MESH
        )

    def d_recv(frm):
        return pltpu.make_async_remote_copy(
            dmsg_ref.at[frm], dtgt.at[frm], d_ss.at[frm], d_rs.at[frm], device_id=node(frm), device_id_type=MESH
        )

    def share(i):
        return pl.ds(pl.multiple_of(i * SHARE, SHARE), SHARE)

    def s_send(to):
        return pltpu.make_async_remote_copy(
            xt_ref.at[:, share(to)], srecv.at[f], s_ss.at[to], s_rs.at[f], device_id=col(to), device_id_type=MESH
        )

    def s_recv(frm):
        return pltpu.make_async_remote_copy(
            xt_ref.at[:, share(frm)], srecv.at[frm], s_ss.at[frm], s_rs.at[frm], device_id=col(frm), device_id_type=MESH
        )

    def z_send(k, to):
        return pltpu.make_async_remote_copy(
            zsend.at[k, to], zrecv.at[k, n], z_ss.at[k, to], z_rs.at[k, n], device_id=node(to), device_id_type=MESH
        )

    def z_recv(k, frm):
        return pltpu.make_async_remote_copy(
            zsend.at[k, frm], zrecv.at[k, frm], z_ss.at[k, frm], z_rs.at[k, frm], device_id=node(frm), device_id_type=MESH
        )

    def g_send(k, to):
        return pltpu.make_async_remote_copy(
            asend.at[k, to], arecv.at[k, f], g_ss.at[k, to], g_rs.at[k, f], device_id=col(to), device_id_type=MESH
        )

    def g_recv(k, frm):
        return pltpu.make_async_remote_copy(
            asend.at[k, frm], arecv.at[k, frm], g_ss.at[k, frm], g_rs.at[k, frm], device_id=col(frm), device_id_type=MESH
        )

    def rows(i):
        return pl.ds(pl.multiple_of(i * C, C), C)

    def b_send(k, to):
        return pltpu.make_async_remote_copy(
            bsend.at[k, rows(to)], brecv.at[k, rows(f)], b_ss.at[k, to], b_rs.at[k, f], device_id=col(to), device_id_type=MESH
        )

    def b_recv(k, frm):
        return pltpu.make_async_remote_copy(
            bsend.at[k, rows(frm)], brecv.at[k, rows(frm)], b_ss.at[k, frm], b_rs.at[k, frm], device_id=col(frm), device_id_type=MESH
        )

    @pl.loop(1, 16)
    def _(step):
        d_send(order(n, step)).start()
        s_send(order(f, step)).start()

    own_self = pltpu.make_async_copy(xt_ref.at[:, share(f)], srecv.at[f], own_sem)
    own_self.start()

    x_copy.wait()

    @pl.loop(0, TILES, unroll=8)
    def _(t):
        xtile[t] = xbuf[:, pl.ds(pl.multiple_of(t * T, T), T)]

    none = jnp.zeros((C, T), BF16)

    def products(d, put):
        for c in range(CAP):
            a = abuf[d, c]
            left = jnp.concatenate([a[: T // 2], a[T // 2 :]], axis=1)
            x = xtile[src_ref[c, d]]
            right = jnp.concatenate(
                [jnp.concatenate([x, none], axis=1), jnp.concatenate([none, x], axis=1)], axis=0
            )
            value = lax.dot_general(left, right, NT, preferred_element_type=F32).astype(BF16)
            for k in range(K):
                put(k, c, value[16 * k : 16 * k + 16])

    @pl.loop(1, 16)
    def _(step):
        d = order(n, step)
        a_copy(step).wait()

        def put(k, c, value):
            zsend[k, d, c] = value

        products(d, put)
        z_send(0, d).start()

    a_copy(0).wait()

    def put_own(k, c, value):
        zrecv[k, n, c] = value

    products(n, put_own)

    dtgt[n] = dmsg_ref[n]
    r32[...] = jnp.zeros_like(r32)
    perm[0] = spread(True)
    perm[1] = spread(False)
    w_copy.wait()

    for part, target in ((0, wt0), (1, wt1)):

        @pl.loop(0, 8)
        def _(i):
            at = pl.ds(pl.multiple_of(i * 128, 128), 128)
            for j in range(8):
                block = wbuf[part, at, 128 * j : 128 * j + 128]
                target[128 * j : 128 * j + 128, at] = block.T

    @pl.loop(1, 16)
    def _(step):
        d_recv(back_order(n, step)).wait_recv()

    low, high = dtgt[0], dtgt[8]
    for s in range(1, 8):
        low, high = low + dtgt[s], high + dtgt[8 + s]
    wanted = jnp.concatenate([low, high], axis=1)
    place = lax.broadcasted_iota(jnp.int32, (TILES, 256), 0) + 1
    onehot[...] = (place == wanted).astype(F32).astype(BF16)

    def self_part():
        own_self.wait()

        @pl.loop(1, 16)
        def _(step):
            s_recv(back_order(f, step)).wait_recv()

        @pl.loop(0, 4)
        def _(i):
            for tq in range(2):
                x = srecv[pl.ds(i * 4, 4), :, 512 * tq : 512 * tq + 512].reshape(256, 512)
                moved = jnp.dot(x, perm[0], preferred_element_type=F32).astype(BF16)
                for k in range(K):
                    selfp[k, pl.ds(pl.multiple_of(i * 256, 256), 256), 128 * tq : 128 * tq + 128] = moved[
                        :, 128 * k : 128 * k + 128
                    ]

        @pl.loop(0, K)
        def _(k):
            hs[k] = jnp.dot(wt1[...], selfp[k], preferred_element_type=F32)

    lane = lax.broadcasted_iota(jnp.int32, (T, 128), 1)

    def chunk(k, is_first, is_last):
        @pl.loop(0, 16)
        def _(step):
            s = back_order(n, step)

            @pl.when(step > 0)
            def _():
                z_recv(k, s).wait_recv()
                if not is_last:
                    z_send(k + 1, order(n, step)).start()

            for c in range(CAP):
                r32[pl.ds(s * 16 + c, 16, stride=256), :] = zrecv[k, s, c].astype(F32)

        @pl.loop(0, 16)
        def _(r):
            x = r32[pl.ds(pl.multiple_of(r * 256, 256), 256), :].astype(BF16)
            g32[pl.ds(r, TILES, stride=16), :] = jnp.dot(onehot[...], x, preferred_element_type=F32)

        @pl.loop(1, 16)
        def _(step):
            to = order(f, step)
            asend[k, to] = g32[pl.ds(pl.multiple_of(to * 128, 128), 128), :].astype(BF16)
            g_send(k, to).start()

        arecv[k, f] = g32[pl.ds(pl.multiple_of(f * 128, 128), 128), :].astype(BF16)

        if is_first:
            self_part()

        @pl.loop(1, 16)
        def _(step):
            g_recv(k, back_order(f, step)).wait_recv()

        for m in range(8):
            a, b = arecv[k, 2 * m].astype(F32), arecv[k, 2 * m + 1].astype(F32)
            first = jnp.where(lane < 64, a, pltpu.roll(b, 64, 1)).astype(BF16)
            second = jnp.where(lane < 64, pltpu.roll(a, 64, 1), b).astype(BF16)
            for tq in range(2):
                cols = slice(128 * m, 128 * m + 128)
                lhs[128 * tq : 128 * tq + 64, cols] = first[64 * tq : 64 * tq + 64]
                lhs[128 * tq + 64 : 128 * tq + 128, cols] = second[64 * tq : 64 * tq + 64]

        act[...] = jnp.maximum(hs[k] + lax.dot_general(wt0[...], lhs[...], NT, preferred_element_type=F32), 0.0)
        total = jnp.sum(act[...] * act[...], axis=0, keepdims=True)
        bsend[k] = (act[...] * lax.rsqrt(total / D + 1e-06)).astype(BF16)

        @pl.loop(1, 16)
        def _(step):
            b_send(k, order(f, step)).start()

        brecv[k, rows(f)] = bsend[k, rows(f)]

    chunk(0, True, False)

    @pl.loop(1, K - 1)
    def _(k):
        chunk(k, False, False)

    chunk(K - 1, False, True)

    @pl.loop(1, 16)
    def _(step):
        for k in range(K):
            b_recv(k, back_order(f, step)).wait_recv()

    @pl.loop(0, 4)
    def _(i):
        for tq in range(2):
            x = jnp.concatenate(
                [brecv[k, pl.ds(pl.multiple_of(i * 256, 256), 256), 128 * tq : 128 * tq + 128] for k in range(K)], axis=1
            )
            moved = jnp.dot(x, perm[1], preferred_element_type=F32).astype(BF16)
            for j in range(4):
                at = pl.multiple_of((i * 4 + j) * SHARE + 512 * tq, 512)
                out_ref[:, pl.ds(at, 512)] = moved[64 * j : 64 * j + 64]

    @pl.loop(1, 16)
    def _(step):
        d_send(order(n, step)).wait_send()
        s_send(order(f, step)).wait_send()
        for k in range(K):
            z_send(k, order(n, step)).wait_send()
            g_send(k, order(f, step)).wait_send()
            b_send(k, order(f, step)).wait_send()


def on_device(features, tile_vals, src_tile, dst_tile, counts, weight):
    n = lax.axis_index("nodes")
    xt = features.T
    src = src_tile.transpose(2, 0, 1).reshape(CAP, N)
    used = lax.broadcasted_iota(jnp.int32, (N, CAP), 1) < counts[0][:, None]
    target = jnp.pad(jnp.where(used, dst_tile[0] + 1, 0), ((0, 0), (0, 16 - CAP)))
    lanes = lax.broadcasted_iota(jnp.int32, (N, 128), 1)
    dmsg = jnp.where(lanes // 16 == n % 8, jnp.tile(target, (1, 8)), 0).reshape(N, 1, 128)

    hbm = pl.BlockSpec(memory_space=pl.ANY)
    vmem = pl.BlockSpec(memory_space=pltpu.VMEM)
    smem = pl.BlockSpec(memory_space=pltpu.SMEM)
    dma = pltpu.SemaphoreType.DMA
    out = pl.pallas_call(
        kernel,
        out_shape=jax.ShapeDtypeStruct((C, TILES * T), BF16),
        in_specs=[smem, vmem, hbm, hbm, hbm],
        out_specs=vmem,
        scratch_shapes=[
            pltpu.VMEM((C, TILES * T), BF16),
            pltpu.VMEM((TILES, C, T), BF16),
            pltpu.VMEM((N, CAP, T, T), BF16),
            pltpu.VMEM((2, D, D), BF16),
            pltpu.VMEM((D, D), BF16),
            pltpu.VMEM((D, D), BF16),
            pltpu.VMEM((K, N, CAP, 16, 128), BF16),
            pltpu.VMEM((K, N, CAP, 16, 128), BF16),
            pltpu.VMEM((N, 1, 128), jnp.int32),
            pltpu.VMEM((16 * 256, 128), F32),
            pltpu.VMEM((TILES * 16, 128), F32),
            pltpu.VMEM((K, F, 128, 128), BF16),
            pltpu.VMEM((K, F, 128, 128), BF16),
            pltpu.VMEM((F, C, SHARE), BF16),
            pltpu.VMEM((K, D, 256), BF16),
            pltpu.VMEM((K, D, 256), F32),
            pltpu.VMEM((256, D), BF16),
            pltpu.VMEM((D, 256), F32),
            pltpu.VMEM((K, D, 256), BF16),
            pltpu.VMEM((K, D, 256), BF16),
            pltpu.VMEM((2, 512, 512), BF16),
            pltpu.VMEM((TILES, 256), BF16),
            dma,
            dma((N,)),
            dma,
            dma,
            dma((N,)),
            dma((N,)),
            dma((F,)),
            dma((F,)),
            dma((K, N)),
            dma((K, N)),
            dma((K, F)),
            dma((K, F)),
            dma((K, F)),
            dma((K, F)),
        ],
        compiler_params=pltpu.CompilerParams(collective_id=1, has_side_effects=True, vmem_limit_bytes=60 * 2**20),
    )(src, dmsg, xt, tile_vals[0], weight)
    return out.T


def solution(mesh):
    return jax.shard_map(
        on_device,
        mesh=mesh,
        in_specs=(
            P("nodes", "feat"),
            P("nodes", None, None, None, None),
            P("nodes", None, None),
            P("nodes", None, None),
            P("nodes", None),
            P(),
        ),
        out_specs=P("nodes", "feat"),
        check_vma=False,
    )
```

time: 217 us -> 124 us (0.57)
  Pallas kernels: 0 us -> 117 us
  waiting for transfers between devices: 93 us -> 0 us
  blocking collectives: 32.5 us -> 0 us
  local copies, waits for them, and re-layouts: 35.7 us -> 4.52 us
  starting transfers between devices: 28.6 us -> 0 us
  matrix products: 23.8 us -> 0 us
    pallas_call x0 -> x1, Pallas kernels: none -> 117 us  [on_device(): pl.pallas_call(kernel, out_shape=jax.ShapeDtypeStruct((C, TILES * T), BF1...]
    all_to_all x4 -> x0, waiting for transfers between devices: 93 us -> none  [the longest x1 67.8 us: on_device(): lax.all_to_all(partial_value, 'nodes', split_axis=0, concat_axis=0, tiled...]
    all_to_all x1 -> x0, blocking collectives: 32.5 us -> none  [on_device(): lax.all_to_all(row_result, 'feat', split_axis=1, concat_axis=0, tiled=True)]
    all_to_all x4 -> x0, starting transfers between devices: 28.6 us -> none  [the longest x1 9.98 us: on_device(): lax.all_to_all(dst_tile[0], 'nodes', split_axis=0, concat_axis=0, tiled=T...]
    dot_general x4 -> x0, matrix products: 23.8 us -> none  [the longest x1 9.83 us: on_device(): jnp.einsum('ncij,ncjd->ncid', tile_vals[0], picked, preferred_element_typ...]
    convert_element_type x2 -> x0, local copies, waits for them, and re-layouts: 11.6 us -> none  [on_device(): aggregate = aggregate.reshape(row_count, col_count).astype(jnp.bfloat16)]
    all_to_all x5 -> x0, local copies, waits for them, and re-layouts: 11 us -> none  [the longest x1 4.49 us: on_device(): lax.all_to_all(partial_value, 'nodes', split_axis=0, concat_axis=0, tiled...]
    reshape x2 -> x0, local copies, waits for them, and re-layouts: 10.1 us -> none  [the longest x1 7.92 us: on_device(): arrived.reshape(owners * slot_count, tile_size * col_count)]
  transfers between devices with their start and end apart: 4 -> 0, of which waited for: 3 -> 0; matrix products, arithmetic and copies ran while one was open for 24% -> 0% of each run, Pallas kernels for 0% -> 0%
where the time goes in v1:
time: 124 us
  Pallas kernels  117 us (94%)
  local copies, waits for them, and re-layouts  4.52 us (4%)
  other arithmetic  1.98 us (2%)
    pallas_call x1, Pallas kernels, on_device(): pl.pallas_call(kernel, out_shape=jax.ShapeDtypeStruct((C, TILES * T), BF1...  117 us
    unnamed x3, local copies, waits for them, and re-layouts  4.42 us

profile of v1, /device:TPU:1, one launch (start us, length us, event | category | flops | bytes accessed | tf_op | source)
XLA Modules:
  0.0 123.9 jit_solution(8119123432014774713)
XLA Ops:
  0.0 0.7 broadcast_add_fusion
  0.7 0.7 bitcast_select_fusion
  1.4 0.1 copy.10
  1.5 1.3 %copy.13 = s32[1,16,12]{1,2,0:T(8,128)} copy(s32[1,16,12]{1,0,2:T(1,128)} %param.8) | data formatting | bytes 1536 | tf_op args[2]
  2.8 0.1 tile.10
  2.9 0.6 compare_select_fusion.dmsg_ref
  3.5 117.4 %shard_map.64 = bf16[64,16384]{1,0:T(8,128)(2,1)} custom-call(s32[12,16]{1,0:T(8,128)} %bitcast.14, s32[16,1,128]{2,1,0:T(1,128)} %compare_select_fusion.dmsg_ref, bf16[64,16384]{1,0:T(8,128)(2,1)} %bitcast.13, bf16[16,12,128,128]{3,2,1,0:T(8,128)(2,1)} %bitcast.12, bf16[2,1024,1024]{2,1,0:T(8,128)(2,1)} %w_ref.1), custom_call_target="tpu_custom_call" | custom-call | tf_op jit(solution)/shard_map/pallas_call | solution.py:365
  120.9 3.0 %copy.15 = bf16[16384,64]{0,1:T(8,128)(2,1)} copy(bf16[16384,64]{0,1:T(8,128)(2,1)} %bitcast.11) | data formatting | bytes 4194304
  (4 shorter events, 0.0 us)

commit v2 on v0

v2 whole, which is shorter than its diff:
```python
import jax
import jax.numpy as jnp
from jax import lax
from jax.experimental import pallas as pl
from jax.experimental.pallas import tpu as pltpu
from jax.sharding import PartitionSpec as P

MESH = pl.DeviceIdType.MESH
BF16, F32 = jnp.bfloat16, jnp.float32
N = 16
F = 16
CAP = 12
T = 128
TILES = 128
C = 64
D = 1024
SHARE = 1024
ROWS = (16, 16, 16, 8, 8)
A, B = 3, 2
LOOK = 2
LANES = 128 * (A + B)

NT = (((1,), (1,)), ((), ()))

FAR = sorted(
    [(dy, dx) for dy in range(4) for dx in range(4) if (dy, dx) != (0, 0)],
    key=lambda o: -(min(o[0], 4 - o[0]) + min(o[1], 4 - o[1])),
)


def node_partner(n, step, sign):
    j = lax.div(step, 2)
    dz = 4 + (2 * lax.rem(j, 2) - 1) * lax.div(j + 1, 2)
    return lax.rem(lax.div(n, 2) + 8 + sign * dz, 8) * 2 + lax.rem(n + step + 1, 2)


def feat_partner(f, offset):
    dy, dx = offset
    return lax.rem(lax.div(f, 4) + dy, 4) * 4 + lax.rem(lax.rem(f, 4) + dx, 4)


def placing(tq):
    lane = lax.broadcasted_iota(jnp.int32, (LANES, 512), 0)
    row = lax.broadcasted_iota(jnp.int32, (LANES, 512), 1)
    tl, h, i = row // 128, (row // 64) % 2, row % 64
    by16 = (i // 16) * 128 + h * 64 + tl * 16 + i % 16
    by8 = A * 128 + ((i - 16 * A) // 8) * 128 + tq * 64 + h * 32 + tl * 8 + i % 8
    return (lane == jnp.where(i < 16 * A, by16, by8)).astype(F32).astype(BF16)


def kernel(
    src_ref,
    dst_ref,
    counts_ref,
    xt_ref,
    a_ref,
    w_ref,
    out_a,
    out_b,
    out_perm,
    xbuf,
    xtile,
    abuf,
    wbuf,
    wt0,
    wt1,
    zsend_a,
    zsend_b,
    zrecv_a,
    zrecv_b,
    turn,
    dmsg,
    dtgt,
    r32,
    g32,
    asend_a,
    asend_b,
    arecv_a,
    arecv_b,
    srecv,
    selfp_a,
    selfp_b,
    hs_a,
    hs_b,
    lhs,
    act,
    bsend_a,
    bsend_b,
    perm,
    onehot,
    xsem,
    asem,
    wsem,
    own_sem,
    perm_sem,
    back_sem,
    d_ss,
    d_rs,
    s_ss,
    s_rs,
    z_ss,
    z_rs,
    g_ss,
    g_rs,
    b_ss,
    b_rs,
):
    n, f = lax.axis_index("nodes"), lax.axis_index("feat")
    across = [feat_partner(f, o) for o in FAR]

    def node(i):
        return (i, f)

    def col(i):
        return (n, i)

    def to_node(step):
        return node_partner(n, step, 1)

    def from_node(step):
        return node_partner(n, step, -1)

    def part(a, b, k):
        return a.at[k] if k < A else b.at[k - A]

    x_copy = pltpu.make_async_copy(xt_ref, xbuf, xsem)
    x_copy.start()

    def a_copy(d):
        return pltpu.make_async_copy(a_ref.at[d], abuf.at[d], asem.at[d])

    @pl.loop(0, 16)
    def _(step):
        a_copy(to_node(step)).start()

    w_copy = pltpu.make_async_copy(w_ref, wbuf, wsem)
    w_copy.start()

    barrier = pltpu.get_barrier_semaphore()

    @pl.loop(0, 15)
    def _(step):
        pl.semaphore_signal(barrier, inc=1, device_id=node(to_node(step)), device_id_type=MESH)

    for to in across:
        pl.semaphore_signal(barrier, inc=1, device_id=col(to), device_id_type=MESH)

    x_copy.wait()

    @pl.loop(0, TILES, unroll=8)
    def _(t):
        xtile[t] = xbuf[:, pl.ds(pl.multiple_of(t * T, T), T)]

    def remote(src, dst, ss, rs, device):
        return pltpu.make_async_remote_copy(src, dst, ss, rs, device_id=device, device_id_type=MESH)

    def all_of(ref, size=1):
        return ref.at[pl.ds(0, 15 * size)]

    def d_send(to):
        return remote(dmsg.at[to], dtgt.at[n], d_ss, d_rs, node(to))

    def d_all():
        return remote(all_of(dmsg), all_of(dtgt), d_ss, d_rs, node(n))

    def share(i):
        return pl.ds(pl.multiple_of(i * SHARE, SHARE), SHARE)

    def s_send(to):
        return remote(xt_ref.at[:, share(to)], srecv.at[f], s_ss, s_rs, col(to))

    def s_all():
        return remote(all_of(srecv), all_of(srecv), s_ss, s_rs, col(f))

    def z_send(k, to):
        src, dst = part(zsend_a, zsend_b, k), part(zrecv_a, zrecv_b, k)
        return remote(src.at[to], dst.at[n], z_ss.at[k], z_rs.at[k, n], node(to))

    def z_recv(k, frm):
        src, dst = part(zsend_a, zsend_b, k), part(zrecv_a, zrecv_b, k)
        return remote(src.at[frm], dst.at[frm], z_ss.at[k], z_rs.at[k, frm], node(frm))

    def z_all(k):
        src, dst = part(zsend_a, zsend_b, k), part(zrecv_a, zrecv_b, k)
        return remote(all_of(src), all_of(dst), z_ss.at[k], z_rs.at[k, n], node(n))

    def g_send(k, to):
        src, dst = part(asend_a, asend_b, k), part(arecv_a, arecv_b, k)
        return remote(src.at[to], dst.at[f], g_ss.at[k], g_rs.at[k], col(to))

    def g_all(k):
        src, dst = part(asend_a, asend_b, k), part(arecv_a, arecv_b, k)
        return remote(all_of(src), all_of(dst), g_ss.at[k], g_rs.at[k], col(f))

    def rows(i):
        return pl.ds(pl.multiple_of(i * C, C), C)

    def b_send(k, to):
        src, dst = part(bsend_a, bsend_b, k), part(out_a, out_b, k)
        return remote(src.at[rows(to)], dst.at[rows(f)], b_ss.at[k], b_rs.at[k], col(to))

    def b_all(k):
        src, dst = part(bsend_a, bsend_b, k), part(out_a, out_b, k)
        return remote(all_of(src, C), all_of(dst, C), b_ss.at[k], b_rs.at[k], col(f))

    def b_own(k):
        src, dst = part(bsend_a, bsend_b, k), part(out_a, out_b, k)
        return pltpu.make_async_copy(src.at[rows(f)], dst.at[rows(f)], back_sem.at[k])

    none = jnp.zeros((C, T), BF16)

    def products(d, to_a, to_b, at):
        kept = None
        for c in range(CAP):
            a = abuf[d, c]
            left = jnp.concatenate([a[: T // 2], a[T // 2 :]], axis=1)
            x = xtile[src_ref[c, 0, d]]
            right = jnp.concatenate(
                [jnp.concatenate([x, none], axis=1), jnp.concatenate([none, x], axis=1)], axis=0
            )
            value = lax.dot_general(left, right, NT, preferred_element_type=F32)
            for k in range(A):
                to_a[k, at, c] = value[16 * k : 16 * k + 16].astype(BF16)
            if c % 2 == 0:
                kept = value
                continue
            for k in range(B):
                rows8 = slice(16 * A + 8 * k, 16 * A + 8 * k + 8)
                to_b[k, at, c // 2] = jnp.concatenate([kept[rows8], value[rows8]], axis=0).astype(BF16)

    def stage_one(step):
        d = to_node(step)
        a_copy(d).wait()
        products(d, zsend_a, zsend_b, d)

    stage_one(0)
    stage_one(1)
    pl.semaphore_wait(barrier, 30)
    for step in range(2):
        z_send(0, to_node(step)).start()

    for to in across:
        s_send(to).start()

    own_self = pltpu.make_async_copy(xt_ref.at[:, share(f)], srecv.at[f], own_sem)
    own_self.start()

    @pl.loop(2, 15)
    def _(step):
        stage_one(step)
        z_send(0, to_node(step)).start()

    turn[...] = jnp.zeros_like(turn)
    for c in range(CAP):
        used = jnp.where(counts_ref[...] > c, dst_ref[c] + 1, 0)
        turn[pl.ds(16 * (n % 8) + c, 1), 0:N] = used.astype(F32)
    turned = turn[...].T
    for d in range(N):
        dmsg[d] = turned[d : d + 1].astype(jnp.int32)

    @pl.loop(0, 15)
    def _(step):
        d_send(to_node(step)).start()

    for k in range(1, LOOK):

        @pl.loop(0, 15)
        def _(step):
            z_send(k, to_node(step)).start()

    a_copy(n).wait()
    products(n, zrecv_a, zrecv_b, n)

    dtgt[n] = dmsg[n]
    r32[...] = jnp.zeros_like(r32)
    perm[0] = placing(0)
    perm[1] = placing(1)
    perm_copy = pltpu.make_async_copy(perm, out_perm, perm_sem)
    perm_copy.start()
    w_copy.wait()

    for which, target in ((0, wt0), (1, wt1)):

        @pl.loop(0, 8)
        def _(i):
            at = pl.ds(pl.multiple_of(i * 128, 128), 128)
            for j in range(8):
                block = wbuf[which, at, 128 * j : 128 * j + 128]
                target[128 * j : 128 * j + 128, at] = block.T

    d_all().wait_recv()
    low, high = dtgt[0], dtgt[8]
    for s in range(1, 8):
        low, high = low + dtgt[s], high + dtgt[8 + s]
    wanted = jnp.concatenate([low, high], axis=1)
    place = lax.broadcasted_iota(jnp.int32, (TILES, 256), 0) + 1
    onehot[...] = (place == wanted).astype(F32).astype(BF16)

    def aggregate(k):
        nr = ROWS[k]
        got = part(zrecv_a, zrecv_b, k)

        def unpack(s):
            if nr == 16:
                for c in range(CAP):
                    r32[pl.ds(s * 16 + c, 16, stride=256), :] = got[s, c].astype(F32)
            else:
                for c in range(0, CAP, 2):
                    both = got[s, c // 2].astype(F32)
                    r32[pl.ds(s * 16 + c, 8, stride=256), :] = both[:8]
                    r32[pl.ds(s * 16 + c + 1, 8, stride=256), :] = both[8:]

        unpack(n)

        @pl.loop(0, 15)
        def _(step):
            s = from_node(step)
            z_recv(k, s).wait_recv()
            if k + LOOK < len(ROWS):
                z_send(k + LOOK, to_node(step)).start()
            unpack(s)

        @pl.loop(0, nr)
        def _(r):
            x = r32[pl.ds(pl.multiple_of(r * 256, 256), 256), :].astype(BF16)
            g32[pl.ds(r, TILES, stride=nr), :] = jnp.dot(onehot[...], x, preferred_element_type=F32)

        def packed(i):
            return g32[pl.ds(pl.multiple_of(i * 8 * nr, 8 * nr), 8 * nr), :].astype(BF16)

        out, mine = part(asend_a, asend_b, k), part(arecv_a, arecv_b, k)
        for to in across:
            out[to] = packed(to)
            g_send(k, to).start()
        mine[f] = packed(f)

    def self_part():
        own_self.wait()
        s_all().wait_recv()

        @pl.loop(0, 4)
        def _(i):
            at = pl.ds(pl.multiple_of(i * 256, 256), 256)
            by8 = [0.0] * B
            for tq in range(2):
                x = srecv[pl.ds(i * 4, 4), :, 512 * tq : 512 * tq + 512].reshape(256, 512)
                moved = lax.dot_general(x, perm[tq], NT, preferred_element_type=F32)
                for k in range(A):
                    selfp_a[k, at, 128 * tq : 128 * tq + 128] = moved[:, 128 * k : 128 * k + 128].astype(BF16)
                for k in range(B):
                    by8[k] = by8[k] + moved[:, 128 * (A + k) : 128 * (A + k) + 128]
            for k in range(B):
                selfp_b[k, at, :] = by8[k].astype(BF16)

        for k in range(A):
            hs_a[k] = jnp.dot(wt1[...], selfp_a[k], preferred_element_type=F32)
        for k in range(B):
            hs_b[k] = jnp.dot(wt1[...], selfp_b[k], preferred_element_type=F32)

    def layer(k):
        nr = ROWS[k]
        wide = 16 * nr
        g_all(k).wait_recv()
        got = part(arecv_a, arecv_b, k)
        lane = lax.broadcasted_iota(jnp.int32, (8 * nr, 128), 1)
        for m in range(8):
            a, b = got[2 * m].astype(F32), got[2 * m + 1].astype(F32)
            first = jnp.where(lane < 64, a, pltpu.roll(b, 64, 1)).astype(BF16)
            second = jnp.where(lane < 64, pltpu.roll(a, 64, 1), b).astype(BF16)
            cols = slice(128 * m, 128 * m + 128)
            for tq in range(2):
                at, of = 8 * nr * tq, slice(4 * nr * tq, 4 * nr * tq + 4 * nr)
                lhs[at : at + 4 * nr, cols] = first[of]
                lhs[at + 4 * nr : at + 8 * nr, cols] = second[of]

        here, away = part(hs_a, hs_b, k), part(bsend_a, bsend_b, k)
        hidden = here[...] + lax.dot_general(wt0[...], lhs[0:wide], NT, preferred_element_type=F32)
        act[:, 0:wide] = jnp.maximum(hidden, 0.0)
        total = jnp.sum(act[:, 0:wide] * act[:, 0:wide], axis=0, keepdims=True)
        away[...] = (act[:, 0:wide] * lax.rsqrt(total / D + 1e-06)).astype(BF16)
        for to in across:
            b_send(k, to).start()
        b_own(k).start()

    for k in range(len(ROWS)):
        aggregate(k)
        if k == 0:
            self_part()
        layer(k)

    perm_copy.wait()
    d_all().wait_send()
    s_all().wait_send()
    for k in range(len(ROWS)):
        z_all(k).wait_send()
        g_all(k).wait_send()
        b_all(k).wait_send()
        b_own(k).wait()
        b_all(k).wait_recv()


def place_kernel(a_ref, b_ref, perm_ref, out_ref):
    for tq in range(2):
        x = [a_ref[k, :, 128 * tq : 128 * tq + 128] for k in range(A)] + [b_ref[k] for k in range(B)]
        moved = jnp.dot(jnp.concatenate(x, axis=1), perm_ref[tq], preferred_element_type=F32).astype(BF16)
        for j in range(4):
            out_ref[:, SHARE * j + 512 * tq : SHARE * j + 512 * tq + 512] = moved[C * j : C * j + C]


def on_device(features, tile_vals, src_tile, dst_tile, counts, weight):
    hbm = pl.BlockSpec(memory_space=pl.ANY)
    vmem = pl.BlockSpec(memory_space=pltpu.VMEM)
    smem = pl.BlockSpec(memory_space=pltpu.SMEM)
    dma = pltpu.SemaphoreType.DMA
    chunks = len(ROWS)

    def both(rows_a, rows_b, kind=BF16):
        return [pltpu.VMEM((A, *rows_a), kind), pltpu.VMEM((B, *rows_b), kind)]

    back_a, back_b, perm = pl.pallas_call(
        kernel,
        out_shape=(
            jax.ShapeDtypeStruct((A, D, 256), BF16),
            jax.ShapeDtypeStruct((B, D, 128), BF16),
            jax.ShapeDtypeStruct((2, LANES, 512), BF16),
        ),
        in_specs=[smem, vmem, vmem, hbm, hbm, hbm],
        out_specs=(hbm, hbm, hbm),
        scratch_shapes=[
            pltpu.VMEM((C, TILES * T), BF16),
            pltpu.VMEM((TILES, C, T), BF16),
            pltpu.VMEM((N, CAP, T, T), BF16),
            pltpu.VMEM((2, D, D), BF16),
            pltpu.VMEM((D, D), BF16),
            pltpu.VMEM((D, D), BF16),
            *both((N, CAP, 16, 128), (N, CAP // 2, 16, 128)),
            *both((N, CAP, 16, 128), (N, CAP // 2, 16, 128)),
            pltpu.VMEM((128, 128), F32),
            pltpu.VMEM((N, 1, 128), jnp.int32),
            pltpu.VMEM((N, 1, 128), jnp.int32),
            pltpu.VMEM((16 * 256, 128), F32),
            pltpu.VMEM((TILES * 16, 128), F32),
            *both((F, 128, 128), (F, 64, 128)),
            *both((F, 128, 128), (F, 64, 128)),
            pltpu.VMEM((F, C, SHARE), BF16),
            *both((D, 256), (D, 128)),
            *both((D, 256), (D, 128), F32),
            pltpu.VMEM((256, D), BF16),
            pltpu.VMEM((D, 256), F32),
            *both((D, 256), (D, 128)),
            pltpu.VMEM((2, LANES, 512), BF16),
            pltpu.VMEM((TILES, 256), BF16),
            dma,
            dma((N,)),
            dma,
            dma,
            dma,
            dma((chunks,)),
            dma,
            dma,
            dma,
            dma,
            dma((chunks,)),
            dma((chunks, N)),
            dma((chunks,)),
            dma((chunks,)),
            dma((chunks,)),
            dma((chunks,)),
        ],
        compiler_params=pltpu.CompilerParams(collective_id=1, has_side_effects=True, vmem_limit_bytes=60 * 2**20),
    )(src_tile.transpose(2, 0, 1), dst_tile.transpose(2, 0, 1), counts, features.T, tile_vals[0], weight)
    out = pl.pallas_call(
        place_kernel,
        grid=(4,),
        out_shape=jax.ShapeDtypeStruct((C, TILES * T), BF16),
        in_specs=[
            pl.BlockSpec((A, 256, 256), lambda i: (0, i, 0)),
            pl.BlockSpec((B, 256, 128), lambda i: (0, i, 0)),
            pl.BlockSpec((2, LANES, 512), lambda i: (0, 0, 0)),
        ],
        out_specs=pl.BlockSpec((C, 4 * SHARE), lambda i: (0, i)),
        compiler_params=pltpu.CompilerParams(vmem_limit_bytes=60 * 2**20),
    )(back_a, back_b, perm)
    return out.T


def solution(mesh):
    return jax.shard_map(
        on_device,
        mesh=mesh,
        in_specs=(
            P("nodes", "feat"),
            P("nodes", None, None, None, None),
            P("nodes", None, None),
            P("nodes", None, None),
            P("nodes", None),
            P(),
        ),
        out_specs=P("nodes", "feat"),
        check_vma=False,
    )
```

time: 217 us -> 111 us (0.51)
  Pallas kernels: 0 us -> 110 us
  waiting for transfers between devices: 93 us -> 0 us
  local copies, waits for them, and re-layouts: 35.7 us -> 0 us
  blocking collectives: 32.5 us -> 0 us
  starting transfers between devices: 28.6 us -> 0 us
  matrix products: 23.8 us -> 0 us
    pallas_call x0 -> x2, Pallas kernels: none -> 110 us  [the longest x1 105 us: on_device(): pl.pallas_call(kernel, out_shape=(jax.ShapeDtypeStruct((A, D, 256), BF16)...]
    all_to_all x4 -> x0, waiting for transfers between devices: 93 us -> none  [the longest x1 67.8 us: on_device(): lax.all_to_all(partial_value, 'nodes', split_axis=0, concat_axis=0, tiled...]
    all_to_all x1 -> x0, blocking collectives: 32.5 us -> none  [on_device(): lax.all_to_all(row_result, 'feat', split_axis=1, concat_axis=0, tiled=True)]
    all_to_all x4 -> x0, starting transfers between devices: 28.6 us -> none  [the longest x1 9.98 us: on_device(): lax.all_to_all(dst_tile[0], 'nodes', split_axis=0, concat_axis=0, tiled=T...]
    dot_general x4 -> x0, matrix products: 23.8 us -> none  [the longest x1 9.83 us: on_device(): jnp.einsum('ncij,ncjd->ncid', tile_vals[0], picked, preferred_element_typ...]
    convert_element_type x2 -> x0, local copies, waits for them, and re-layouts: 11.6 us -> none  [on_device(): aggregate = aggregate.reshape(row_count, col_count).astype(jnp.bfloat16)]
    all_to_all x5 -> x0, local copies, waits for them, and re-layouts: 11 us -> none  [the longest x1 4.49 us: on_device(): lax.all_to_all(partial_value, 'nodes', split_axis=0, concat_axis=0, tiled...]
    reshape x2 -> x0, local copies, waits for them, and re-layouts: 10.1 us -> none  [the longest x1 7.92 us: on_device(): arrived.reshape(owners * slot_count, tile_size * col_count)]
  transfers between devices with their start and end apart: 4 -> 0, of which waited for: 3 -> 0; matrix products, arithmetic and copies ran while one was open for 24% -> 0% of each run, Pallas kernels for 0% -> 0%
where the time goes in v2:
time: 111 us; the launch traced here: 110 us
  Pallas kernels  110 us (99%)
    pallas_call x1, Pallas kernels, on_device(): pl.pallas_call(kernel, out_shape=(jax.ShapeDtypeStruct((A, D, 256), BF16)...  105 us
    pallas_call x1, Pallas kernels, on_device(): pl.pallas_call(place_kernel, grid=(4,), out_shape=jax.ShapeDtypeStruct((C...  5.34 us

profile of v2, /device:TPU:1, one launch (start us, length us, event | category | flops | bytes accessed | tf_op | source)
XLA Modules:
  0.0 110.2 jit_solution(12528993322366654719)
XLA Ops:
  0.0 104.9 %shard_map.64 = (bf16[3,1024,256]{2,1,0:T(8,128)(2,1)}, bf16[2,1024,128]{2,1,0:T(8,128)(2,1)}, bf16[2,640,512]{2,1,0:T(8,128)(2,1)}) custom-call(s32[12,1,16]{2,1,0:T(1,128)} %bitcast.7, s32[12,1,16]{2,1,0:T(1,128)} %bitcast.8, s32[1,16]{1,0:T(1,128)} %counts_ref.1, bf16[64,16384]{1,0:T(8,128)(2,1)} %bitcast.6, bf16[16,12,128,128]{3,2,1,0:T(8,128)(2,1)} %bitcast.5, ...), custom_call_target="tpu_custom_call" | custom-call | tf_op jit(solution)/shard_map/pallas_call | solution.py:420
  104.9 5.3 %shard_map.65 = bf16[64,16384]{1,0:T(8,128)(2,1)} custom-call(bf16[3,1024,256]{2,1,0:T(8,128)(2,1)} %get-tuple-element.8.a_ref, bf16[2,1024,128]{2,1,0:T(8,128)(2,1)} %get-tuple-element.9.b_ref, bf16[2,640,512]{2,1,0:T(8,128)(2,1)} %get-tuple-element.10.perm_ref), custom_call_target="tpu_custom_call" | custom-call | tf_op jit(solution)/shard_map/pallas_call | solution.py:472

commit v3 on v2

--- a/solution.py
+++ b/solution.py
@@ -19,6 +19,9 @@
 A, B = 3, 2
 LOOK = 2
 LANES = 128 * (A + B)
+SCHEDULE = (
+    ("sum", 0), ("layer", 0), ("sum", 1), ("layer", 1), ("sum", 2), ("sum", 3), ("layer", 2), ("layer", 3), ("sum", 4), ("layer", 4),
+)
 
 NT = (((1,), (1,)), ((), ()))
 
@@ -382,11 +385,13 @@
             b_send(k, to).start()
         b_own(k).start()
 
-    for k in range(len(ROWS)):
-        aggregate(k)
-        if k == 0:
-            self_part()
-        layer(k)
+    for step, k in SCHEDULE:
+        if step == "sum":
+            aggregate(k)
+        else:
+            if k == 0:
+                self_part()
+            layer(k)
 
     perm_copy.wait()
     d_all().wait_send()
@@ -399,12 +404,40 @@
         b_all(k).wait_recv()
 
 
-def place_kernel(a_ref, b_ref, perm_ref, out_ref):
-    for tq in range(2):
-        x = [a_ref[k, :, 128 * tq : 128 * tq + 128] for k in range(A)] + [b_ref[k] for k in range(B)]
-        moved = jnp.dot(jnp.concatenate(x, axis=1), perm_ref[tq], preferred_element_type=F32).astype(BF16)
-        for j in range(4):
-            out_ref[:, SHARE * j + 512 * tq : SHARE * j + 512 * tq + 512] = moved[C * j : C * j + C]
+def place_kernel(a_ref, b_ref, perm_ref, out_ref, abuf, bbuf, pbuf, obuf, a_sem, b_sem, p_sem, o_sem):
+    def fetch(i):
+        at = pl.ds(256 * i, 256)
+        return (
+            pltpu.make_async_copy(a_ref.at[:, at], abuf.at[i], a_sem.at[i]),
+            pltpu.make_async_copy(b_ref.at[:, at], bbuf.at[i], b_sem.at[i]),
+        )
+
+    def fetch_perm(tq):
+        return pltpu.make_async_copy(perm_ref.at[tq], pbuf.at[tq], p_sem.at[tq])
+
+    def store(i):
+        return pltpu.make_async_copy(obuf.at[i], out_ref.at[:, pl.ds(4 * SHARE * i, 4 * SHARE)], o_sem.at[i])
+
+    fetch_perm(0).start()
+    for i in range(4):
+        for copy in fetch(i):
+            copy.start()
+        if i == 0:
+            fetch_perm(1).start()
+    for i in range(4):
+        for tq in range(2):
+            if i == 0:
+                fetch_perm(tq).wait()
+            if tq == 0:
+                for copy in fetch(i):
+                    copy.wait()
+            x = [abuf[i, k, :, 128 * tq : 128 * tq + 128] for k in range(A)] + [bbuf[i, k] for k in range(B)]
+            moved = jnp.dot(jnp.concatenate(x, axis=1), pbuf[tq], preferred_element_type=F32).astype(BF16)
+            for j in range(4):
+                obuf[i, :, SHARE * j + 512 * tq : SHARE * j + 512 * tq + 512] = moved[C * j : C * j + C]
+        store(i).start()
+    for i in range(4):
+        store(i).wait()
 
 
 def on_device(features, tile_vals, src_tile, dst_tile, counts, weight):
@@ -471,14 +504,19 @@
     )(src_tile.transpose(2, 0, 1), dst_tile.transpose(2, 0, 1), counts, features.T, tile_vals[0], weight)
     out = pl.pallas_call(
         place_kernel,
-        grid=(4,),
         out_shape=jax.ShapeDtypeStruct((C, TILES * T), BF16),
-        in_specs=[
-            pl.BlockSpec((A, 256, 256), lambda i: (0, i, 0)),
-            pl.BlockSpec((B, 256, 128), lambda i: (0, i, 0)),
-            pl.BlockSpec((2, LANES, 512), lambda i: (0, 0, 0)),
+        in_specs=[hbm, hbm, hbm],
+        out_specs=hbm,
+        scratch_shapes=[
+            pltpu.VMEM((4, A, 256, 256), BF16),
+            pltpu.VMEM((4, B, 256, 128), BF16),
+            pltpu.VMEM((2, LANES, 512), BF16),
+            pltpu.VMEM((4, C, 4 * SHARE), BF16),
+            dma((4,)),
+            dma((4,)),
+            dma((2,)),
+            dma((4,)),
         ],
-        out_specs=pl.BlockSpec((C, 4 * SHARE), lambda i: (0, i)),
         compiler_params=pltpu.CompilerParams(vmem_limit_bytes=60 * 2**20),
     )(back_a, back_b, perm)
     return out.T

time: 111 us -> 105 us (0.946)
  Pallas kernels: 110 us -> 105 us
    pallas_call x1, Pallas kernels: 105 us -> 100 us  [on_device(): pl.pallas_call(kernel, out_shape=(jax.ShapeDtypeStruct((A, D, 256), BF16)...]
where the time goes in v3:
time: 105 us
  Pallas kernels  105 us (100%)
    pallas_call x1, Pallas kernels, on_device(): pl.pallas_call(kernel, out_shape=(jax.ShapeDtypeStruct((A, D, 256), BF16)...  100 us
    pallas_call x1, Pallas kernels, on_device(): pl.pallas_call(place_kernel, out_shape=jax.ShapeDtypeStruct((C, TILES * T...  4.82 us

profile of v3, /device:TPU:1, one launch (start us, length us, event | category | flops | bytes accessed | tf_op | source)
XLA Modules:
  0.0 105.3 jit_solution(20336610536649798)
XLA Ops:
  0.0 100.3 %shard_map.64 = (bf16[3,1024,256]{2,1,0:T(8,128)(2,1)}, bf16[2,1024,128]{2,1,0:T(8,128)(2,1)}, bf16[2,640,512]{2,1,0:T(8,128)(2,1)}) custom-call(s32[12,1,16]{2,1,0:T(1,128)} %bitcast.7, s32[12,1,16]{2,1,0:T(1,128)} %bitcast.8, s32[1,16]{1,0:T(1,128)} %counts_ref.1, bf16[64,16384]{1,0:T(8,128)(2,1)} %bitcast.6, bf16[16,12,128,128]{3,2,1,0:T(8,128)(2,1)} %bitcast.5, ...), custom_call_target="tpu_custom_call" | custom-call | tf_op jit(solution)/shard_map/pallas_call | solution.py:453
  100.3 4.8 %shard_map.65 = bf16[64,16384]{1,0:T(8,128)(2,1)} custom-call(bf16[3,1024,256]{2,1,0:T(8,128)(2,1)} %get-tuple-element.8.a_ref, bf16[2,1024,128]{2,1,0:T(8,128)(2,1)} %get-tuple-element.9.b_ref, bf16[2,640,512]{2,1,0:T(8,128)(2,1)} %get-tuple-element.10.perm_ref), custom_call_target="tpu_custom_call" | custom-call | tf_op jit(solution)/shard_map/pallas_call | solution.py:505

commit v4 on v3

--- a/solution.py
+++ b/solution.py
@@ -237,10 +237,8 @@
         products(d, zsend_a, zsend_b, d)
 
     stage_one(0)
-    stage_one(1)
     pl.semaphore_wait(barrier, 30)
-    for step in range(2):
-        z_send(0, to_node(step)).start()
+    z_send(0, to_node(0)).start()
 
     for to in across:
         s_send(to).start()
@@ -248,7 +246,7 @@
     own_self = pltpu.make_async_copy(xt_ref.at[:, share(f)], srecv.at[f], own_sem)
     own_self.start()
 
-    @pl.loop(2, 15)
+    @pl.loop(1, 15)
     def _(step):
         stage_one(step)
         z_send(0, to_node(step)).start()
@@ -323,10 +321,17 @@
                 z_send(k + LOOK, to_node(step)).start()
             unpack(s)
 
-        @pl.loop(0, nr)
-        def _(r):
-            x = r32[pl.ds(pl.multiple_of(r * 256, 256), 256), :].astype(BF16)
-            g32[pl.ds(r, TILES, stride=nr), :] = jnp.dot(onehot[...], x, preferred_element_type=F32)
+        def rows_of(r):
+            return r32[pl.ds(pl.multiple_of(r * 256, 256), 256), :]
+
+        @pl.loop(0, nr // 4)
+        def _(quarter):
+            for pair in range(2):
+                r = quarter * 4 + 2 * pair
+                x = jnp.concatenate([rows_of(r), rows_of(r + 1)], axis=1).astype(BF16)
+                sums = jnp.dot(onehot[...], x, preferred_element_type=F32)
+                g32[pl.ds(r, TILES, stride=nr), :] = sums[:, :128]
+                g32[pl.ds(r + 1, TILES, stride=nr), :] = sums[:, 128:]
 
         def packed(i):
             return g32[pl.ds(pl.multiple_of(i * 8 * nr, 8 * nr), 8 * nr), :].astype(BF16)
@@ -377,9 +382,13 @@
                 lhs[at + 4 * nr : at + 8 * nr, cols] = second[of]
 
         here, away = part(hs_a, hs_b, k), part(bsend_a, bsend_b, k)
-        hidden = here[...] + lax.dot_general(wt0[...], lhs[0:wide], NT, preferred_element_type=F32)
-        act[:, 0:wide] = jnp.maximum(hidden, 0.0)
-        total = jnp.sum(act[:, 0:wide] * act[:, 0:wide], axis=0, keepdims=True)
+        total = jnp.zeros((1, wide), F32)
+        for at in range(0, D, D // 2):
+            half = slice(at, at + D // 2)
+            hidden = here[half] + lax.dot_general(wt0[half], lhs[0:wide], NT, preferred_element_type=F32)
+            active = jnp.maximum(hidden, 0.0)
+            act[half, 0:wide] = active
+            total = total + jnp.sum(active * active, axis=0, keepdims=True)
         away[...] = (act[:, 0:wide] * lax.rsqrt(total / D + 1e-06)).astype(BF16)
         for to in across:
             b_send(k, to).start()

time: 105 us -> 104 us (level)
  Pallas kernels: 105 us -> 103 us
    pallas_call x1, Pallas kernels: 100 us -> 98.6 us  [on_device(): pl.pallas_call(kernel, out_shape=(jax.ShapeDtypeStruct((A, D, 256), BF16)...]
where the time goes in v4:
time: 104 us
  Pallas kernels  103 us (99%)
    pallas_call x1, Pallas kernels, on_device(): pl.pallas_call(kernel, out_shape=(jax.ShapeDtypeStruct((A, D, 256), BF16)...  98.6 us
    pallas_call x1, Pallas kernels, on_device(): pl.pallas_call(place_kernel, out_shape=jax.ShapeDtypeStruct((C, TILES * T...  4.82 us

profile of v4, /device:TPU:1, one launch (start us, length us, event | category | flops | bytes accessed | tf_op | source)
XLA Modules:
  0.0 103.6 jit_solution(11891332694319262232)
XLA Ops:
  0.0 98.6 %shard_map.64 = (bf16[3,1024,256]{2,1,0:T(8,128)(2,1)}, bf16[2,1024,128]{2,1,0:T(8,128)(2,1)}, bf16[2,640,512]{2,1,0:T(8,128)(2,1)}) custom-call(s32[12,1,16]{2,1,0:T(1,128)} %bitcast.7, s32[12,1,16]{2,1,0:T(1,128)} %bitcast.8, s32[1,16]{1,0:T(1,128)} %counts_ref.1, bf16[64,16384]{1,0:T(8,128)(2,1)} %bitcast.6, bf16[16,12,128,128]{3,2,1,0:T(8,128)(2,1)} %bitcast.5, ...), custom_call_target="tpu_custom_call" | custom-call | tf_op jit(solution)/shard_map/pallas_call | solution.py:462
  98.6 4.8 %shard_map.65 = bf16[64,16384]{1,0:T(8,128)(2,1)} custom-call(bf16[3,1024,256]{2,1,0:T(8,128)(2,1)} %get-tuple-element.8.a_ref, bf16[2,1024,128]{2,1,0:T(8,128)(2,1)} %get-tuple-element.9.b_ref, bf16[2,640,512]{2,1,0:T(8,128)(2,1)} %get-tuple-element.10.perm_ref), custom_call_target="tpu_custom_call" | custom-call | tf_op jit(solution)/shard_map/pallas_call | solution.py:514

commit v5 on v4

--- a/solution.py
+++ b/solution.py
@@ -18,7 +18,9 @@
 ROWS = (16, 16, 16, 8, 8)
 A, B = 3, 2
 LOOK = 2
+LAST = len(ROWS) - 1
 LANES = 128 * (A + B)
+MOST = 128 * LAST
 SCHEDULE = (
     ("sum", 0), ("layer", 0), ("sum", 1), ("layer", 1), ("sum", 2), ("sum", 3), ("layer", 2), ("layer", 3), ("sum", 4), ("layer", 4),
 )
@@ -58,8 +60,8 @@
     xt_ref,
     a_ref,
     w_ref,
-    out_a,
-    out_b,
+    out_most,
+    out_last,
     out_perm,
     xbuf,
     xtile,
@@ -89,6 +91,9 @@
     act,
     bsend_a,
     bsend_b,
+    brecv_a,
+    brecv_b,
+    most,
     perm,
     onehot,
     xsem,
@@ -96,6 +101,7 @@
     wsem,
     own_sem,
     perm_sem,
+    most_sem,
     back_sem,
     d_ss,
     d_rs,
@@ -126,6 +132,9 @@
     def part(a, b, k):
         return a.at[k] if k < A else b.at[k - A]
 
+    def back(k):
+        return out_last if k == LAST else part(brecv_a, brecv_b, k)
+
     x_copy = pltpu.make_async_copy(xt_ref, xbuf, xsem)
     x_copy.start()
 
@@ -199,15 +208,15 @@
         return pl.ds(pl.multiple_of(i * C, C), C)
 
     def b_send(k, to):
-        src, dst = part(bsend_a, bsend_b, k), part(out_a, out_b, k)
+        src, dst = part(bsend_a, bsend_b, k), back(k)
         return remote(src.at[rows(to)], dst.at[rows(f)], b_ss.at[k], b_rs.at[k], col(to))
 
     def b_all(k):
-        src, dst = part(bsend_a, bsend_b, k), part(out_a, out_b, k)
+        src, dst = part(bsend_a, bsend_b, k), back(k)
         return remote(all_of(src, C), all_of(dst, C), b_ss.at[k], b_rs.at[k], col(f))
 
     def b_own(k):
-        src, dst = part(bsend_a, bsend_b, k), part(out_a, out_b, k)
+        src, dst = part(bsend_a, bsend_b, k), back(k)
         return pltpu.make_async_copy(src.at[rows(f)], dst.at[rows(f)], back_sem.at[k])
 
     none = jnp.zeros((C, T), BF16)
@@ -276,7 +285,7 @@
     r32[...] = jnp.zeros_like(r32)
     perm[0] = placing(0)
     perm[1] = placing(1)
-    perm_copy = pltpu.make_async_copy(perm, out_perm, perm_sem)
+    perm_copy = pltpu.make_async_copy(perm.at[:, pl.ds(MOST, 128)], out_perm, perm_sem)
     perm_copy.start()
     w_copy.wait()
 
@@ -389,9 +398,11 @@
             active = jnp.maximum(hidden, 0.0)
             act[half, 0:wide] = active
             total = total + jnp.sum(active * active, axis=0, keepdims=True)
-        away[...] = (act[:, 0:wide] * lax.rsqrt(total / D + 1e-06)).astype(BF16)
+        scale = lax.rsqrt(total / D + 1e-06)
         for to in across:
+            away[rows(to)] = (act[rows(to), 0:wide] * scale).astype(BF16)
             b_send(k, to).start()
+        away[rows(f)] = (act[rows(f), 0:wide] * scale).astype(BF16)
         b_own(k).start()
 
     for step, k in SCHEDULE:
@@ -402,6 +413,25 @@
                 self_part()
             layer(k)
 
+    for k in range(LAST):
+        b_own(k).wait()
+        b_all(k).wait_recv()
+
+    def most_copy(i):
+        at = pl.ds(pl.multiple_of(i * 4 * SHARE, 4 * SHARE), 4 * SHARE)
+        return pltpu.make_async_copy(most.at[:, at], out_most.at[:, at], most_sem.at[i])
+
+    @pl.loop(0, 4)
+    def _(i):
+        of = pl.ds(pl.multiple_of(i * 256, 256), 256)
+        for tq in range(2):
+            x = [brecv_a[k, of, 128 * tq : 128 * tq + 128] for k in range(A)] + [brecv_b[k, of, :] for k in range(B - 1)]
+            moved = jnp.dot(jnp.concatenate(x, axis=1), perm[tq, 0:MOST], preferred_element_type=F32).astype(BF16)
+            for j in range(4):
+                at = pl.multiple_of((i * 4 + j) * SHARE + 512 * tq, 512)
+                most[:, pl.ds(at, 512)] = moved[C * j : C * j + C]
+        most_copy(i).start()
+
     perm_copy.wait()
     d_all().wait_send()
     s_all().wait_send()
@@ -409,41 +439,37 @@
         z_all(k).wait_send()
         g_all(k).wait_send()
         b_all(k).wait_send()
-        b_own(k).wait()
-        b_all(k).wait_recv()
-
-
-def place_kernel(a_ref, b_ref, perm_ref, out_ref, abuf, bbuf, pbuf, obuf, a_sem, b_sem, p_sem, o_sem):
+    for i in range(4):
+        most_copy(i).wait()
+    b_own(LAST).wait()
+    b_all(LAST).wait_recv()
+
+
+def place_kernel(most_ref, last_ref, perm_ref, out_ref, mbuf, lbuf, pbuf, obuf, m_sem, l_sem, p_sem, o_sem):
+    def block(i):
+        return pl.ds(4 * SHARE * i, 4 * SHARE)
+
     def fetch(i):
-        at = pl.ds(256 * i, 256)
-        return (
-            pltpu.make_async_copy(a_ref.at[:, at], abuf.at[i], a_sem.at[i]),
-            pltpu.make_async_copy(b_ref.at[:, at], bbuf.at[i], b_sem.at[i]),
-        )
-
-    def fetch_perm(tq):
-        return pltpu.make_async_copy(perm_ref.at[tq], pbuf.at[tq], p_sem.at[tq])
+        return pltpu.make_async_copy(most_ref.at[:, block(i)], mbuf.at[i], m_sem.at[i])
 
     def store(i):
-        return pltpu.make_async_copy(obuf.at[i], out_ref.at[:, pl.ds(4 * SHARE * i, 4 * SHARE)], o_sem.at[i])
-
-    fetch_perm(0).start()
+        return pltpu.make_async_copy(obuf.at[i], out_ref.at[:, block(i)], o_sem.at[i])
+
+    fetch_perm = pltpu.make_async_copy(perm_ref, pbuf, p_sem)
+    fetch_last = pltpu.make_async_copy(last_ref, lbuf, l_sem)
+    fetch_perm.start()
+    fetch_last.start()
     for i in range(4):
-        for copy in fetch(i):
-            copy.start()
-        if i == 0:
-            fetch_perm(1).start()
+        fetch(i).start()
+    fetch_perm.wait()
+    fetch_last.wait()
     for i in range(4):
+        fetch(i).wait()
         for tq in range(2):
-            if i == 0:
-                fetch_perm(tq).wait()
-            if tq == 0:
-                for copy in fetch(i):
-                    copy.wait()
-            x = [abuf[i, k, :, 128 * tq : 128 * tq + 128] for k in range(A)] + [bbuf[i, k] for k in range(B)]
-            moved = jnp.dot(jnp.concatenate(x, axis=1), pbuf[tq], preferred_element_type=F32).astype(BF16)
+            moved = jnp.dot(lbuf[256 * i : 256 * i + 256], pbuf[tq], preferred_element_type=F32)
             for j in range(4):
-                obuf[i, :, SHARE * j + 512 * tq : SHARE * j + 512 * tq + 512] = moved[C * j : C * j + C]
+                at = slice(SHARE * j + 512 * tq, SHARE * j + 512 * tq + 512)
+                obuf[i, :, at] = (mbuf[i, :, at].astype(F32) + moved[C * j : C * j + C]).astype(BF16)
         store(i).start()
     for i in range(4):
         store(i).wait()
@@ -459,12 +485,12 @@
     def both(rows_a, rows_b, kind=BF16):
         return [pltpu.VMEM((A, *rows_a), kind), pltpu.VMEM((B, *rows_b), kind)]
 
-    back_a, back_b, perm = pl.pallas_call(
+    most, last, perm = pl.pallas_call(
         kernel,
         out_shape=(
-            jax.ShapeDtypeStruct((A, D, 256), BF16),
-            jax.ShapeDtypeStruct((B, D, 128), BF16),
-            jax.ShapeDtypeStruct((2, LANES, 512), BF16),
+            jax.ShapeDtypeStruct((C, TILES * T), BF16),
+            jax.ShapeDtypeStruct((D, 128), BF16),
+            jax.ShapeDtypeStruct((2, 128, 512), BF16),
         ),
         in_specs=[smem, vmem, vmem, hbm, hbm, hbm],
         out_specs=(hbm, hbm, hbm),
@@ -490,6 +516,9 @@
             pltpu.VMEM((256, D), BF16),
             pltpu.VMEM((D, 256), F32),
             *both((D, 256), (D, 128)),
+            pltpu.VMEM((A, D, 256), BF16),
+            pltpu.VMEM((B - 1, D, 128), BF16),
+            pltpu.VMEM((C, TILES * T), BF16),
             pltpu.VMEM((2, LANES, 512), BF16),
             pltpu.VMEM((TILES, 256), BF16),
             dma,
@@ -497,6 +526,7 @@
             dma,
             dma,
             dma,
+            dma((4,)),
             dma((chunks,)),
             dma,
             dma,
@@ -517,17 +547,17 @@
         in_specs=[hbm, hbm, hbm],
         out_specs=hbm,
         scratch_shapes=[
-            pltpu.VMEM((4, A, 256, 256), BF16),
-            pltpu.VMEM((4, B, 256, 128), BF16),
-            pltpu.VMEM((2, LANES, 512), BF16),
+            pltpu.VMEM((4, C, 4 * SHARE), BF16),
+            pltpu.VMEM((D, 128), BF16),
+            pltpu.VMEM((2, 128, 512), BF16),
             pltpu.VMEM((4, C, 4 * SHARE), BF16),
             dma((4,)),
-            dma((4,)),
-            dma((2,)),
+            dma,
+            dma,
             dma((4,)),
         ],
         compiler_params=pltpu.CompilerParams(vmem_limit_bytes=60 * 2**20),
-    )(back_a, back_b, perm)
+    )(most, last, perm)
     return out.T
 
 

time: 104 us -> 102 us (0.981)
    pallas_call x1, Pallas kernels: 4.82 us -> 3.53 us  [on_device(): pl.pallas_call(place_kernel, out_shape=jax.ShapeDtypeStruct((C, TILES * T...]
where the time goes in v5:
time: 102 us
  Pallas kernels  102 us (100%)
    pallas_call x1, Pallas kernels, on_device(): pl.pallas_call(kernel, out_shape=(jax.ShapeDtypeStruct((C, TILES * T), BF...  98.6 us
    pallas_call x1, Pallas kernels, on_device(): pl.pallas_call(place_kernel, out_shape=jax.ShapeDtypeStruct((C, TILES * T...  3.53 us

profile of v5, /device:TPU:1, one launch (start us, length us, event | category | flops | bytes accessed | tf_op | source)
XLA Modules:
  0.0 102.1 jit_solution(3003953940185768567)
XLA Ops:
  0.0 98.6 %shard_map.64 = (bf16[64,16384]{1,0:T(8,128)(2,1)}, bf16[1024,128]{1,0:T(8,128)(2,1)}, bf16[2,128,512]{2,1,0:T(8,128)(2,1)}) custom-call(s32[12,1,16]{2,1,0:T(1,128)} %bitcast.7, s32[12,1,16]{2,1,0:T(1,128)} %bitcast.8, s32[1,16]{1,0:T(1,128)} %counts_ref.1, bf16[64,16384]{1,0:T(8,128)(2,1)} %bitcast.6, bf16[16,12,128,128]{3,2,1,0:T(8,128)(2,1)} %bitcast.5, ...), custom_call_target="tpu_custom_call" | custom-call | tf_op jit(solution)/shard_map/pallas_call | solution.py:488
  98.6 3.5 %shard_map.65 = bf16[64,16384]{1,0:T(8,128)(2,1)} custom-call(bf16[64,16384]{1,0:T(8,128)(2,1)} %get-tuple-element.8.most_ref, bf16[1024,128]{1,0:T(8,128)(2,1)} %get-tuple-element.9.last_ref, bf16[2,128,512]{2,1,0:T(8,128)(2,1)} %get-tuple-element.10.perm_ref), custom_call_target="tpu_custom_call" | custom-call | tf_op jit(solution)/shard_map/pallas_call | solution.py:544

commit v6 on v5

--- a/solution.py
+++ b/solution.py
@@ -21,17 +21,9 @@
 LAST = len(ROWS) - 1
 LANES = 128 * (A + B)
 MOST = 128 * LAST
-SCHEDULE = (
-    ("sum", 0), ("layer", 0), ("sum", 1), ("layer", 1), ("sum", 2), ("sum", 3), ("layer", 2), ("layer", 3), ("sum", 4), ("layer", 4),
-)
+CHUNKS = [(0, a) for a in range(A)] + [(1, b) for b in range(B)]
 
 NT = (((1,), (1,)), ((), ()))
-
-FAR = sorted(
-    [(dy, dx) for dy in range(4) for dx in range(4) if (dy, dx) != (0, 0)],
-    key=lambda o: -(min(o[0], 4 - o[0]) + min(o[1], 4 - o[1])),
-)
-
 
 def node_partner(n, step, sign):
     j = lax.div(step, 2)
@@ -115,7 +107,6 @@
     b_rs,
 ):
     n, f = lax.axis_index("nodes"), lax.axis_index("feat")
-    across = [feat_partner(f, o) for o in FAR]
 
     def node(i):
         return (i, f)
@@ -130,10 +121,17 @@
         return node_partner(n, step, -1)
 
     def part(a, b, k):
-        return a.at[k] if k < A else b.at[k - A]
+        return (b if k[0] else a).at[k[1]]
+
+    def num(k):
+        return A * k[0] + k[1]
+
+    def across(step):
+        s = step + lax.div(step, 10)
+        return feat_partner(f, (2 + lax.div(s, 4), 2 + lax.rem(s, 4)))
 
     def back(k):
-        return out_last if k == LAST else part(brecv_a, brecv_b, k)
+        return out_last if k == "last" else part(brecv_a, brecv_b, k)
 
     x_copy = pltpu.make_async_copy(xt_ref, xbuf, xsem)
     x_copy.start()
@@ -154,8 +152,9 @@
     def _(step):
         pl.semaphore_signal(barrier, inc=1, device_id=node(to_node(step)), device_id_type=MESH)
 
-    for to in across:
-        pl.semaphore_signal(barrier, inc=1, device_id=col(to), device_id_type=MESH)
+    @pl.loop(0, 15)
+    def _(step):
+        pl.semaphore_signal(barrier, inc=1, device_id=col(across(step)), device_id_type=MESH)
 
     x_copy.wait()
 
@@ -186,38 +185,43 @@
 
     def z_send(k, to):
         src, dst = part(zsend_a, zsend_b, k), part(zrecv_a, zrecv_b, k)
-        return remote(src.at[to], dst.at[n], z_ss.at[k], z_rs.at[k, n], node(to))
+        return remote(src.at[to], dst.at[n], z_ss.at[num(k)], z_rs.at[num(k), n], node(to))
 
     def z_recv(k, frm):
         src, dst = part(zsend_a, zsend_b, k), part(zrecv_a, zrecv_b, k)
-        return remote(src.at[frm], dst.at[frm], z_ss.at[k], z_rs.at[k, frm], node(frm))
+        return remote(src.at[frm], dst.at[frm], z_ss.at[num(k)], z_rs.at[num(k), frm], node(frm))
 
     def z_all(k):
         src, dst = part(zsend_a, zsend_b, k), part(zrecv_a, zrecv_b, k)
-        return remote(all_of(src), all_of(dst), z_ss.at[k], z_rs.at[k, n], node(n))
+        return remote(all_of(src), all_of(dst), z_ss.at[num(k)], z_rs.at[num(k), n], node(n))
 
     def g_send(k, to):
         src, dst = part(asend_a, asend_b, k), part(arecv_a, arecv_b, k)
-        return remote(src.at[to], dst.at[f], g_ss.at[k], g_rs.at[k], col(to))
+        return remote(src.at[to], dst.at[f], g_ss.at[num(k)], g_rs.at[num(k)], col(to))
 
     def g_all(k):
         src, dst = part(asend_a, asend_b, k), part(arecv_a, arecv_b, k)
-        return remote(all_of(src), all_of(dst), g_ss.at[k], g_rs.at[k], col(f))
+        return remote(all_of(src), all_of(dst), g_ss.at[num(k)], g_rs.at[num(k)], col(f))
 
     def rows(i):
         return pl.ds(pl.multiple_of(i * C, C), C)
 
+    def b_ends(k):
+        last = k == "last"
+        chunk = (1, B - 1) if last else k
+        return part(bsend_a, bsend_b, chunk), back(k), num(chunk)
+
     def b_send(k, to):
-        src, dst = part(bsend_a, bsend_b, k), back(k)
-        return remote(src.at[rows(to)], dst.at[rows(f)], b_ss.at[k], b_rs.at[k], col(to))
+        src, dst, c = b_ends(k)
+        return remote(src.at[rows(to)], dst.at[rows(f)], b_ss.at[c], b_rs.at[c], col(to))
 
     def b_all(k):
-        src, dst = part(bsend_a, bsend_b, k), back(k)
-        return remote(all_of(src, C), all_of(dst, C), b_ss.at[k], b_rs.at[k], col(f))
+        src, dst, c = b_ends(k)
+        return remote(all_of(src, C), all_of(dst, C), b_ss.at[c], b_rs.at[c], col(f))
 
     def b_own(k):
-        src, dst = part(bsend_a, bsend_b, k), back(k)
-        return pltpu.make_async_copy(src.at[rows(f)], dst.at[rows(f)], back_sem.at[k])
+        src, dst, c = b_ends(k)
+        return pltpu.make_async_copy(src.at[rows(f)], dst.at[rows(f)], back_sem.at[c])
 
     none = jnp.zeros((C, T), BF16)
 
@@ -247,10 +251,11 @@
 
     stage_one(0)
     pl.semaphore_wait(barrier, 30)
-    z_send(0, to_node(0)).start()
-
-    for to in across:
-        s_send(to).start()
+    z_send((0, 0), to_node(0)).start()
+
+    @pl.loop(0, 15)
+    def _(step):
+        s_send(across(step)).start()
 
     own_self = pltpu.make_async_copy(xt_ref.at[:, share(f)], srecv.at[f], own_sem)
     own_self.start()
@@ -258,7 +263,7 @@
     @pl.loop(1, 15)
     def _(step):
         stage_one(step)
-        z_send(0, to_node(step)).start()
+        z_send((0, 0), to_node(step)).start()
 
     turn[...] = jnp.zeros_like(turn)
     for c in range(CAP):
@@ -276,7 +281,7 @@
 
         @pl.loop(0, 15)
         def _(step):
-            z_send(k, to_node(step)).start()
+            z_send((0, k), to_node(step)).start()
 
     a_copy(n).wait()
     products(n, zrecv_a, zrecv_b, n)
@@ -307,7 +312,7 @@
     onehot[...] = (place == wanted).astype(F32).astype(BF16)
 
     def aggregate(k):
-        nr = ROWS[k]
+        nr = (16, 8)[k[0]]
         got = part(zrecv_a, zrecv_b, k)
 
         def unpack(s):
@@ -326,8 +331,16 @@
         def _(step):
             s = from_node(step)
             z_recv(k, s).wait_recv()
-            if k + LOOK < len(ROWS):
-                z_send(k + LOOK, to_node(step)).start()
+            if k[0] == 0:
+
+                @pl.when(k[1] + LOOK < A)
+                def _():
+                    z_send((0, k[1] + LOOK), to_node(step)).start()
+
+                @pl.when(k[1] + LOOK >= A)
+                def _():
+                    z_send((1, k[1] + LOOK - A), to_node(step)).start()
+
             unpack(s)
 
         def rows_of(r):
@@ -346,9 +359,13 @@
             return g32[pl.ds(pl.multiple_of(i * 8 * nr, 8 * nr), 8 * nr), :].astype(BF16)
 
         out, mine = part(asend_a, asend_b, k), part(arecv_a, arecv_b, k)
-        for to in across:
+
+        @pl.loop(0, 15)
+        def _(step):
+            to = across(step)
             out[to] = packed(to)
             g_send(k, to).start()
+
         mine[f] = packed(f)
 
     def self_part():
@@ -375,7 +392,7 @@
             hs_b[k] = jnp.dot(wt1[...], selfp_b[k], preferred_element_type=F32)
 
     def layer(k):
-        nr = ROWS[k]
+        nr = (16, 8)[k[0]]
         wide = 16 * nr
         g_all(k).wait_recv()
         got = part(arecv_a, arecv_b, k)
@@ -399,21 +416,52 @@
             act[half, 0:wide] = active
             total = total + jnp.sum(active * active, axis=0, keepdims=True)
         scale = lax.rsqrt(total / D + 1e-06)
-        for to in across:
-            away[rows(to)] = (act[rows(to), 0:wide] * scale).astype(BF16)
-            b_send(k, to).start()
-        away[rows(f)] = (act[rows(f), 0:wide] * scale).astype(BF16)
-        b_own(k).start()
-
-    for step, k in SCHEDULE:
-        if step == "sum":
-            aggregate(k)
+
+        def send_back(k):
+            @pl.loop(0, 15)
+            def _(step):
+                to = across(step)
+                away[rows(to)] = (act[rows(to), 0:wide] * scale).astype(BF16)
+                b_send(k, to).start()
+
+            away[rows(f)] = (act[rows(f), 0:wide] * scale).astype(BF16)
+            b_own(k).start()
+
+        if k[0] == 0:
+            send_back(k)
         else:
-            if k == 0:
-                self_part()
-            layer(k)
-
-    for k in range(LAST):
+
+            @pl.when(k[1] < B - 1)
+            def _():
+                send_back((1, 0))
+
+            @pl.when(k[1] == B - 1)
+            def _():
+                send_back("last")
+
+    @pl.loop(0, 10)
+    def _(step):
+        @pl.when((step == 0) | (step == 2) | (step == 4))
+        def _():
+            aggregate((0, lax.div(step, 2)))
+
+        @pl.when(step == 0)
+        def _():
+            self_part()
+
+        @pl.when((step == 1) | (step == 3) | (step == 6))
+        def _():
+            layer((0, lax.div(step, 3)))
+
+        @pl.when((step == 5) | (step == 8))
+        def _():
+            aggregate((1, lax.div(step - 5, 3)))
+
+        @pl.when((step == 7) | (step == 9))
+        def _():
+            layer((1, lax.div(step - 7, 2)))
+
+    for k in CHUNKS[:LAST]:
         b_own(k).wait()
         b_all(k).wait_recv()
 
@@ -435,14 +483,14 @@
     perm_copy.wait()
     d_all().wait_send()
     s_all().wait_send()
-    for k in range(len(ROWS)):
+    for k in CHUNKS:
         z_all(k).wait_send()
         g_all(k).wait_send()
-        b_all(k).wait_send()
+        b_all("last" if k == CHUNKS[LAST] else k).wait_send()
     for i in range(4):
         most_copy(i).wait()
-    b_own(LAST).wait()
-    b_all(LAST).wait_recv()
+    b_own("last").wait()
+    b_all("last").wait_recv()
 
 
 def place_kernel(most_ref, last_ref, perm_ref, out_ref, mbuf, lbuf, pbuf, obuf, m_sem, l_sem, p_sem, o_sem):

time: 102 us -> 104 us (1.020); the launches traced: 102 us -> 103 us
  no operation moved by 1% of the time
where the time goes in v6:
time: 104 us; the launch traced here: 103 us
  Pallas kernels  103 us (99%)
    pallas_call x1, Pallas kernels, on_device(): pl.pallas_call(kernel, out_shape=(jax.ShapeDtypeStruct((C, TILES * T), BF...  99.5 us
    pallas_call x1, Pallas kernels, on_device(): pl.pallas_call(place_kernel, out_shape=jax.ShapeDtypeStruct((C, TILES * T...  3.52 us

profile of v6, /device:TPU:1, one launch (start us, length us, event | category | flops | bytes accessed | tf_op | source)
XLA Modules:
  0.0 103.1 jit_solution(16138107897449756459)
XLA Ops:
  0.0 99.5 %shard_map.64 = (bf16[64,16384]{1,0:T(8,128)(2,1)}, bf16[1024,128]{1,0:T(8,128)(2,1)}, bf16[2,128,512]{2,1,0:T(8,128)(2,1)}) custom-call(s32[12,1,16]{2,1,0:T(1,128)} %bitcast.7, s32[12,1,16]{2,1,0:T(1,128)} %bitcast.8, s32[1,16]{1,0:T(1,128)} %counts_ref.1, bf16[64,16384]{1,0:T(8,128)(2,1)} %bitcast.6, bf16[16,12,128,128]{3,2,1,0:T(8,128)(2,1)} %bitcast.5, ...), custom_call_target="tpu_custom_call" | custom-call | tf_op jit(solution)/shard_map/pallas_call | solution.py:536
  99.5 3.5 %shard_map.65 = bf16[64,16384]{1,0:T(8,128)(2,1)} custom-call(bf16[64,16384]{1,0:T(8,128)(2,1)} %get-tuple-element.8.most_ref, bf16[1024,128]{1,0:T(8,128)(2,1)} %get-tuple-element.9.last_ref, bf16[2,128,512]{2,1,0:T(8,128)(2,1)} %get-tuple-element.10.perm_ref), custom_call_target="tpu_custom_call" | custom-call | tf_op jit(solution)/shard_map/pallas_call | solution.py:592

commit v7 on v5

--- a/solution.py
+++ b/solution.py
@@ -34,9 +34,13 @@
 
 
 def node_partner(n, step, sign):
-    j = lax.div(step, 2)
-    dz = 4 + (2 * lax.rem(j, 2) - 1) * lax.div(j + 1, 2)
-    return lax.rem(lax.div(n, 2) + 8 + sign * dz, 8) * 2 + lax.rem(n + step + 1, 2)
+    if isinstance(step, int):
+        j = step // 2
+        dz = 4 + (2 * (j % 2) - 1) * ((j + 1) // 2)
+    else:
+        j = lax.div(step, 2)
+        dz = 4 + (2 * lax.rem(j, 2) - 1) * lax.div(j + 1, 2)
+    return lax.rem(lax.div(n, 2) + (8 + sign * dz), 8) * 2 + lax.rem(n + (step + 1), 2)
 
 
 def feat_partner(f, offset):
@@ -126,8 +130,8 @@
     def to_node(step):
         return node_partner(n, step, 1)
 
-    def from_node(step):
-        return node_partner(n, step, -1)
+    receivers = [to_node(step) for step in range(15)]
+    senders = [node_partner(n, step, -1) for step in range(15)]
 
     def part(a, b, k):
         return a.at[k] if k < A else b.at[k - A]
@@ -150,9 +154,8 @@
 
     barrier = pltpu.get_barrier_semaphore()
 
-    @pl.loop(0, 15)
-    def _(step):
-        pl.semaphore_signal(barrier, inc=1, device_id=node(to_node(step)), device_id_type=MESH)
+    for to in receivers:
+        pl.semaphore_signal(barrier, inc=1, device_id=node(to), device_id_type=MESH)
 
     for to in across:
         pl.semaphore_signal(barrier, inc=1, device_id=col(to), device_id_type=MESH)
@@ -268,15 +271,12 @@
     for d in range(N):
         dmsg[d] = turned[d : d + 1].astype(jnp.int32)
 
-    @pl.loop(0, 15)
-    def _(step):
-        d_send(to_node(step)).start()
+    for to in receivers:
+        d_send(to).start()
 
     for k in range(1, LOOK):
-
-        @pl.loop(0, 15)
-        def _(step):
-            z_send(k, to_node(step)).start()
+        for to in receivers:
+            z_send(k, to).start()
 
     a_copy(n).wait()
     products(n, zrecv_a, zrecv_b, n)
@@ -322,12 +322,10 @@
 
         unpack(n)
 
-        @pl.loop(0, 15)
-        def _(step):
-            s = from_node(step)
+        for s, to in zip(senders, receivers):
             z_recv(k, s).wait_recv()
             if k + LOOK < len(ROWS):
-                z_send(k + LOOK, to_node(step)).start()
+                z_send(k + LOOK, to).start()
             unpack(s)
 
         def rows_of(r):

time: 102 us -> 102 us (level)
  no operation moved by 1% of the time
where the time goes in v7:
time: 102 us
  Pallas kernels  102 us (100%)
    pallas_call x1, Pallas kernels, on_device(): pl.pallas_call(kernel, out_shape=(jax.ShapeDtypeStruct((C, TILES * T), BF...  98.1 us
    pallas_call x1, Pallas kernels, on_device(): pl.pallas_call(place_kernel, out_shape=jax.ShapeDtypeStruct((C, TILES * T...  3.52 us

profile of v7, /device:TPU:1, one launch (start us, length us, event | category | flops | bytes accessed | tf_op | source)
XLA Modules:
  0.0 101.8 jit_solution(17063667434994853637)
XLA Ops:
  0.0 98.1 %shard_map.64 = (bf16[64,16384]{1,0:T(8,128)(2,1)}, bf16[1024,128]{1,0:T(8,128)(2,1)}, bf16[2,128,512]{2,1,0:T(8,128)(2,1)}) custom-call(s32[12,1,16]{2,1,0:T(1,128)} %bitcast.7, s32[12,1,16]{2,1,0:T(1,128)} %bitcast.8, s32[1,16]{1,0:T(1,128)} %counts_ref.1, bf16[64,16384]{1,0:T(8,128)(2,1)} %bitcast.6, bf16[16,12,128,128]{3,2,1,0:T(8,128)(2,1)} %bitcast.5, ...), custom_call_target="tpu_custom_call" | custom-call | tf_op jit(solution)/shard_map/pallas_call | solution.py:486
  98.1 3.5 %shard_map.65 = bf16[64,16384]{1,0:T(8,128)(2,1)} custom-call(bf16[64,16384]{1,0:T(8,128)(2,1)} %get-tuple-element.8.most_ref, bf16[1024,128]{1,0:T(8,128)(2,1)} %get-tuple-element.9.last_ref, bf16[2,128,512]{2,1,0:T(8,128)(2,1)} %get-tuple-element.10.perm_ref), custom_call_target="tpu_custom_call" | custom-call | tf_op jit(solution)/shard_map/pallas_call | solution.py:542

commit v8 on v5

--- a/solution.py
+++ b/solution.py
@@ -15,14 +15,15 @@
 C = 64
 D = 1024
 SHARE = 1024
-ROWS = (16, 16, 16, 8, 8)
-A, B = 3, 2
+ROWS = (16, 16, 8, 8, 8, 8)
+A, B = 2, 4
 LOOK = 2
 LAST = len(ROWS) - 1
 LANES = 128 * (A + B)
 MOST = 128 * LAST
 SCHEDULE = (
-    ("sum", 0), ("layer", 0), ("sum", 1), ("layer", 1), ("sum", 2), ("sum", 3), ("layer", 2), ("layer", 3), ("sum", 4), ("layer", 4),
+    ("sum", 0), ("layer", 0), ("sum", 1), ("sum", 2), ("layer", 1), ("sum", 3), ("layer", 2),
+    ("sum", 4), ("layer", 3), ("layer", 4), ("sum", 5), ("layer", 5),
 )
 
 NT = (((1,), (1,)), ((), ()))

time: 102 us -> 100 us (0.980); the launches traced: 102 us -> 98.8 us
  Pallas kernels: 102 us -> 98.6 us
    pallas_call x1, Pallas kernels: 98.6 us -> 95.1 us  [on_device(): pl.pallas_call(kernel, out_shape=(jax.ShapeDtypeStruct((C, TILES * T), BF...]
where the time goes in v8:
time: 100 us; the launch traced here: 98.8 us
  Pallas kernels  98.6 us (99%)
    pallas_call x1, Pallas kernels, on_device(): pl.pallas_call(kernel, out_shape=(jax.ShapeDtypeStruct((C, TILES * T), BF...  95.1 us
    pallas_call x1, Pallas kernels, on_device(): pl.pallas_call(place_kernel, out_shape=jax.ShapeDtypeStruct((C, TILES * T...  3.53 us

profile of v8, /device:TPU:1, one launch (start us, length us, event | category | flops | bytes accessed | tf_op | source)
XLA Modules:
  0.0 98.8 jit_solution(17107040767234390349)
XLA Ops:
  0.0 95.1 %shard_map.64 = (bf16[64,16384]{1,0:T(8,128)(2,1)}, bf16[1024,128]{1,0:T(8,128)(2,1)}, bf16[2,128,512]{2,1,0:T(8,128)(2,1)}) custom-call(s32[12,1,16]{2,1,0:T(1,128)} %bitcast.7, s32[12,1,16]{2,1,0:T(1,128)} %bitcast.8, s32[1,16]{1,0:T(1,128)} %counts_ref.1, bf16[64,16384]{1,0:T(8,128)(2,1)} %bitcast.6, bf16[16,12,128,128]{3,2,1,0:T(8,128)(2,1)} %bitcast.5, ...), custom_call_target="tpu_custom_call" | custom-call | tf_op jit(solution)/shard_map/pallas_call | solution.py:489
  95.1 3.5 %shard_map.65 = bf16[64,16384]{1,0:T(8,128)(2,1)} custom-call(bf16[64,16384]{1,0:T(8,128)(2,1)} %get-tuple-element.8.most_ref, bf16[1024,128]{1,0:T(8,128)(2,1)} %get-tuple-element.9.last_ref, bf16[2,128,512]{2,1,0:T(8,128)(2,1)} %get-tuple-element.10.perm_ref), custom_call_target="tpu_custom_call" | custom-call | tf_op jit(solution)/shard_map/pallas_call | solution.py:545

commit v9 on v8

--- a/solution.py
+++ b/solution.py
@@ -23,7 +23,7 @@
 MOST = 128 * LAST
 SCHEDULE = (
     ("sum", 0), ("layer", 0), ("sum", 1), ("sum", 2), ("layer", 1), ("sum", 3), ("layer", 2),
-    ("sum", 4), ("layer", 3), ("layer", 4), ("sum", 5), ("layer", 5),
+    ("sum", 4), ("layer", 3), ("sum", 5), ("layer", 4), ("layer", 5),
 )
 
 NT = (((1,), (1,)), ((), ()))

time: 100 us -> 98.9 us (0.989); the launches traced: 98.8 us -> 98.8 us
  no operation moved by 1% of the time
where the time goes in v9:
time: 98.9 us; the launch traced here: 98.8 us
  Pallas kernels  98.8 us (100%)
    pallas_call x1, Pallas kernels, on_device(): pl.pallas_call(kernel, out_shape=(jax.ShapeDtypeStruct((C, TILES * T), BF...  95.3 us
    pallas_call x1, Pallas kernels, on_device(): pl.pallas_call(place_kernel, out_shape=jax.ShapeDtypeStruct((C, TILES * T...  3.53 us

profile of v9, /device:TPU:1, one launch (start us, length us, event | category | flops | bytes accessed | tf_op | source)
XLA Modules:
  0.0 98.8 jit_solution(5529510606620618618)
XLA Ops:
  0.0 95.3 %shard_map.64 = (bf16[64,16384]{1,0:T(8,128)(2,1)}, bf16[1024,128]{1,0:T(8,128)(2,1)}, bf16[2,128,512]{2,1,0:T(8,128)(2,1)}) custom-call(s32[12,1,16]{2,1,0:T(1,128)} %bitcast.7, s32[12,1,16]{2,1,0:T(1,128)} %bitcast.8, s32[1,16]{1,0:T(1,128)} %counts_ref.1, bf16[64,16384]{1,0:T(8,128)(2,1)} %bitcast.6, bf16[16,12,128,128]{3,2,1,0:T(8,128)(2,1)} %bitcast.5, ...), custom_call_target="tpu_custom_call" | custom-call | tf_op jit(solution)/shard_map/pallas_call | solution.py:489
  95.3 3.5 %shard_map.65 = bf16[64,16384]{1,0:T(8,128)(2,1)} custom-call(bf16[64,16384]{1,0:T(8,128)(2,1)} %get-tuple-element.8.most_ref, bf16[1024,128]{1,0:T(8,128)(2,1)} %get-tuple-element.9.last_ref, bf16[2,128,512]{2,1,0:T(8,128)(2,1)} %get-tuple-element.10.perm_ref), custom_call_target="tpu_custom_call" | custom-call | tf_op jit(solution)/shard_map/pallas_call | solution.py:545
